TPU v7x, 256 devices: a whole 4x4x8 slice. The times are simulated.
256 devices in a mesh: dp: 32 (over x, z), tensor: 8 (over y, core).
Axes of the slice: x: 4, y: 4, z: 8, core: 2. Of those that a mesh axis runs over, the one named last changes fastest.
Arguments:
- queries: bfloat16 [24576, 4096], P('dp', 'tensor'), may hold values from -6 to 6
- keys: bfloat16 [24576, 2048], P('dp', 'tensor'), may hold values from -6 to 6
- values: bfloat16 [24576, 2048], P('dp', 'tensor'), may hold values from -6 to 6
- out_grad: bfloat16 [24576, 4096], P('dp', 'tensor'), may hold values from -6 to 6
- query_weight: bfloat16 [4608, 4096], P(None, 'tensor'), may hold values from -0.09375 to 0.09375
- parents: int32 [192], P('dp'), may hold values from -1 to 186, as said below
- lengths: int32 [192], P('dp'), may hold values from 1 to 128
Outputs:
- key_grad: bfloat16 [24576, 2048], P('dp', 'tensor')
- value_grad: bfloat16 [24576, 2048], P('dp', 'tensor')
- hidden_grad: bfloat16 [4608, 24576], P('tensor', 'dp')
Inputs may be any that keep to these rules, and one draw needn't show every extreme that they name: Node i is stored on dp index i div 6. Only the first node of each dp index can have children; every parent is such a node, a chain of parents has at most three links, and some node is a root.
All inputs are finite; a program needn't handle non-finite values.
Results may differ from a plain program's by a relative error of at most 0.02.
Values may be sent and summed in bfloat16 or wider, within the bound.
No kernel may reach another device: no remote copies, remote signals or barrier semaphores. Data moves between devices by JAX's collectives and lax.ppermute only.
A program may use at most 128 MiB of HBM per device.

v0:
```python
import functools

import jax
import jax.numpy as jnp
from jax import lax
from jax.experimental import pallas as pl
from jax.experimental.pallas import tpu as pltpu
from jax.sharding import PartitionSpec as P

HEAD = 128
SOFTCAP = 50
BLOCK = 128
QSCALAR = 144
META = 16
NX = 4
F32, BF16 = jnp.float32, jnp.bfloat16


def dot(a, b, ca, cb):
    return lax.dot_general(a, b, (((ca,), (cb,)), ((), ())), preferred_element_type=F32)


def pack_kernel(node_count, parents, lengths, k_ref, v_ref, a_ref, b_ref):
    a_ref[0:BLOCK] = k_ref[:, :HEAD]
    a_ref[BLOCK : 2 * BLOCK] = v_ref[:, :HEAD]
    b_ref[0:BLOCK] = k_ref[:, HEAD:]
    b_ref[BLOCK : 2 * BLOCK] = v_ref[:, HEAD:]
    parent = parents[0]
    link = jnp.where(parent >= 0, lax.div(jnp.maximum(parent, 0), node_count), -1)
    lane = lax.broadcasted_iota(jnp.int32, (META, HEAD), 1)
    meta = jnp.where(lane == 0, link, lengths[0])
    a_ref[2 * BLOCK :] = meta.astype(F32).astype(BF16)


def main_kernel(node_count, nz, parents, lengths, spot, q_ref, k_ref, v_ref, g_ref, w_ref, *refs):
    parts, refs = refs[: 5 + nz], refs[5 + nz :]
    kg_ref, vg_ref, out_ref = refs[:3]
    terms, refs = refs[3 : 8 + nz], refs[8 + nz :]
    far_a, far_b, acc_a, acc_b, send_a, send_b, qg_ref, meta_v, meta_s, sem, out_sem, meta_sem = refs
    half = nz // 2
    step = pl.program_id(0)
    pieces = [(0, nz), (nz, nz), (3 * nz, nz), (2 * nz, half), (2 * nz + half, half)]
    ranges = [(0, at, size) for at, size in pieces] + [(1, sz * NX, NX) for sz in range(nz)]

    def copies_in():
        return [
            pltpu.make_async_copy(part, (far_a, far_b)[h].at[pl.ds(at, size)], sem.at[i])
            for i, (part, (h, at, size)) in enumerate(zip(parts, ranges))
        ]

    def copies_out():
        return [
            pltpu.make_async_copy((send_a, send_b)[h].at[pl.ds(at, size)], term, out_sem.at[i])
            for i, (term, (h, at, size)) in enumerate(zip(terms, ranges))
        ]

    @pl.when(step == 0)
    def _():
        for copy in copies_in():
            copy.start()
        acc_a[...] = jnp.zeros_like(acc_a)
        acc_b[...] = jnp.zeros_like(acc_b)
        for copy in copies_in():
            copy.wait()
        meta = jnp.max(far_a[:, 2 * BLOCK :, :].astype(F32), axis=1)
        meta_v[...] = meta.astype(jnp.int32)
        copy = pltpu.make_async_copy(meta_v, meta_s, meta_sem)
        copy.start()
        copy.wait()

    @pl.when(step < node_count)
    def _():
        attend(
            node_count, nz, step, parents, lengths, spot, meta_s, (far_a, far_b), (acc_a, acc_b),
            q_ref, k_ref, v_ref, g_ref, kg_ref, vg_ref, qg_ref,
        )

    @pl.when(step == node_count - 1)
    def _():
        send_a[...] = acc_a[...].astype(BF16)
        send_b[...] = acc_b[...].astype(BF16)
        for copy in copies_out():
            copy.start()

    @pl.when(step >= node_count)
    def _():
        out_ref[...] = dot(w_ref[...], qg_ref[...], 1, 0).astype(BF16)

    @pl.when(step == pl.num_programs(0) - 1)
    def _():
        for copy in copies_out():
            copy.wait()


def attend(
    node_count, nz, node, parents, lengths, spot, meta_s, far_refs, acc_refs,
    q_ref, k_ref, v_ref, g_ref, kg_ref, vg_ref, qg_ref,
):
    scale = QSCALAR ** (-0.5)
    x_me, z_me = spot[0], spot[1]
    here = pl.ds(pl.multiple_of(node * BLOCK, BLOCK), BLOCK)

    def place(link):
        safe = jnp.maximum(link, 0)
        lx = lax.div(safe, nz)
        sx = lax.rem(x_me - lx + NX, NX)
        sz = lax.rem(z_me - (safe - lx * nz) + nz, nz)
        return sx * nz + sz, sz * NX + sx

    parent = parents[node]
    link = jnp.where(parent >= 0, lax.div(jnp.maximum(parent, 0), node_count), -1)
    slots, lens = [], [lengths[node]]
    for _ in range(3):
        slot_a, slot_b = place(link)
        slots.append((slot_a, slot_b))
        lens.append(jnp.where(link >= 0, meta_s[slot_a, 1], 0))
        link = jnp.where(link >= 0, meta_s[slot_a, 0], -1)

    cols = 2 * BLOCK
    key_row = lax.broadcasted_iota(jnp.int32, (BLOCK, cols), 0)
    query_col = lax.broadcasted_iota(jnp.int32, (BLOCK, cols), 1)
    query_col = jnp.where(query_col >= BLOCK, query_col - BLOCK, query_col)
    live = lax.broadcasted_iota(jnp.int32, (BLOCK, HEAD), 0) < lens[0]
    masks = [(key_row < lens[0]) & (key_row <= query_col)] + [key_row < m for m in lens[1:]]

    for h in range(2):
        far = far_refs[h]
        acc = acc_refs[h]
        lo, mid, hi = 2 * h * HEAD, (2 * h + 1) * HEAD, (2 * h + 2) * HEAD
        q = jnp.concatenate([q_ref[:, lo:mid], q_ref[:, mid:hi]], axis=0)
        zero = jnp.zeros((), BF16)
        g = jnp.concatenate(
            [jnp.where(live, g_ref[:, lo:mid], zero), jnp.where(live, g_ref[:, mid:hi], zero)], axis=0
        )
        at = slice(h * HEAD, (h + 1) * HEAD)
        keys = [k_ref[:, at]] + [far[s[h], 0:BLOCK, :] for s in slots]
        vals = [v_ref[:, at]] + [far[s[h], BLOCK : 2 * BLOCK, :] for s in slots]
        squash, weight, grad = [], [], []
        total = jnp.zeros((1, cols), F32)
        mixed = jnp.zeros((1, cols), F32)
        for b in range(4):
            t = jnp.tanh(dot(keys[b], q, 1, 1) * (scale / SOFTCAP))
            e = jnp.where(masks[b], jnp.exp(SOFTCAP * t), 0.0)
            d = dot(vals[b], g, 1, 1)
            total += jnp.sum(e, axis=0, keepdims=True)
            mixed += jnp.sum(e * d, axis=0, keepdims=True)
            squash.append(t)
            weight.append(e)
            grad.append(d)
        inverse = 1.0 / total
        delta = mixed * inverse
        query_grad = jnp.zeros((HEAD, cols), F32)
        for b in range(4):
            p = weight[b] * inverse
            ds = (p * (grad[b] - delta) * (scale - scale * (squash[b] * squash[b]))).astype(BF16)
            dk = dot(ds, q, 1, 0)
            dv = dot(p.astype(BF16), g, 1, 0)
            query_grad += dot(keys[b], ds, 0, 0)
            if b == 0:
                kg_ref[:, at] = dk.astype(BF16)
                vg_ref[:, at] = dv.astype(BF16)

                @pl.when(node == 0)
                def _():
                    acc[0, 0:BLOCK, :] += dk
                    acc[0, BLOCK:, :] += dv
            else:
                slot = slots[b - 1][h]
                acc[slot, 0:BLOCK, :] += dk
                acc[slot, BLOCK:, :] += dv
        qg_ref[lo:mid, here] = query_grad[:, :BLOCK].astype(BF16)
        qg_ref[mid:hi, here] = query_grad[:, BLOCK:].astype(BF16)


def local(queries, keys, values, out_grad, query_weight, parents, lengths, *, dp):
    node_count = parents.shape[0]
    rows, cols = queries.shape
    kv_cols = keys.shape[1]
    width = query_weight.shape[0]
    nz = dp // NX
    half = nz // 2

    def send(array, dx, dz):
        pairs = [
            (x * nz + z, ((x + dx) % NX) * nz + (z + dz) % nz) for x in range(NX) for z in range(nz)
        ]
        return lax.ppermute(array, "dp", pairs)

    def add(*terms):
        return sum(t.astype(F32) for t in terms).astype(BF16)

    me = lax.axis_index("dp")
    spot = jnp.stack([me // nz, me % nz]).astype(jnp.int32)
    smem = pl.BlockSpec(memory_space=pltpu.SMEM)
    pack_a, pack_b = pl.pallas_call(
        functools.partial(pack_kernel, node_count),
        grid=(1,),
        in_specs=[smem, smem] + [pl.BlockSpec((BLOCK, kv_cols), lambda i: (0, 0))] * 2,
        out_specs=[
            pl.BlockSpec((2 * BLOCK + META, HEAD), lambda i: (0, 0)),
            pl.BlockSpec((2 * BLOCK, HEAD), lambda i: (0, 0)),
        ],
        out_shape=[
            jax.ShapeDtypeStruct((2 * BLOCK + META, HEAD), BF16),
            jax.ShapeDtypeStruct((2 * BLOCK, HEAD), BF16),
        ],
        name="pack",
    )(parents, lengths, keys, values)

    a1, a7, a2, a6 = (send(pack_a, 0, s) for s in (1, -1, 2, -2))
    b1, b3, b2 = (send(pack_b, s, 0) for s in (1, -1, 2))
    near_b = jnp.stack([pack_b, b1, b2, b3])
    a34 = send(jnp.stack([a1, a2]), 0, 2)
    a5 = send(a7, 0, -2)
    rings = [near_b] + [None] * (nz - 1)
    for s in range(1, half + 1):
        rings[s] = send(rings[s - 1], 0, 1)
        if s < half:
            rings[nz - s] = send(rings[(nz - s + 1) % nz], 0, -1)
    near_a = jnp.concatenate([jnp.stack([pack_a, a1, a2]), a34, jnp.stack([a5, a6, a7])])
    after, before = send(near_a, 1, 0), send(near_a, -1, 0)
    parts = [near_a, after, before, send(after[:half], 1, 0), send(before[half:], -1, 0)] + rings

    any_spec = pl.BlockSpec(memory_space=pl.ANY)
    tiles = 8
    tile = width // tiles
    node_map = lambda i: (jnp.minimum(i, node_count - 1), 0)
    tile_map = lambda i: (jnp.maximum(i - node_count, 0), 0)
    sizes = [nz, nz, nz, half, half] + [NX] * nz
    outs = pl.pallas_call(
        functools.partial(main_kernel, node_count, nz),
        grid=(node_count + tiles,),
        in_specs=[
            smem,
            smem,
            smem,
            pl.BlockSpec((BLOCK, cols), node_map),
            pl.BlockSpec((BLOCK, kv_cols), node_map),
            pl.BlockSpec((BLOCK, kv_cols), node_map),
            pl.BlockSpec((BLOCK, cols), node_map),
            pl.BlockSpec((tile, cols), tile_map),
        ]
        + [any_spec] * (5 + nz),
        out_specs=[
            pl.BlockSpec((BLOCK, kv_cols), node_map),
            pl.BlockSpec((BLOCK, kv_cols), node_map),
            pl.BlockSpec((tile, rows), tile_map),
        ]
        + [any_spec] * (5 + nz),
        out_shape=[
            jax.ShapeDtypeStruct((rows, kv_cols), BF16),
            jax.ShapeDtypeStruct((rows, kv_cols), BF16),
            jax.ShapeDtypeStruct((width, rows), BF16),
        ]
        + [jax.ShapeDtypeStruct((size, 2 * BLOCK, HEAD), BF16) for size in sizes],
        scratch_shapes=[
            pltpu.VMEM((dp, 2 * BLOCK + META, HEAD), BF16),
            pltpu.VMEM((dp, 2 * BLOCK, HEAD), BF16),
            pltpu.VMEM((dp, 2 * BLOCK, HEAD), F32),
            pltpu.VMEM((dp, 2 * BLOCK, HEAD), F32),
            pltpu.VMEM((dp, 2 * BLOCK, HEAD), BF16),
            pltpu.VMEM((dp, 2 * BLOCK, HEAD), BF16),
            pltpu.VMEM((cols, rows), BF16),
            pltpu.VMEM((dp, HEAD), jnp.int32),
            pltpu.SMEM((dp, HEAD), jnp.int32),
            pltpu.SemaphoreType.DMA((5 + nz,)),
            pltpu.SemaphoreType.DMA((5 + nz,)),
            pltpu.SemaphoreType.DMA,
        ],
        compiler_params=pltpu.CompilerParams(vmem_limit_bytes=58 * 1024 * 1024),
        name="attention",
    )(parents, lengths, spot, queries, keys, values, out_grad, query_weight, *parts)
    key_grad, value_grad, hidden = outs[:3]
    own, prev, succ, far_low, far_high = outs[3:8]
    terms = outs[8:]

    hidden_grad = lax.psum_scatter(hidden, "tensor", scatter_dimension=0, tiled=True)

    low_a, high_a = send(far_low, -1, 0), send(far_high, 1, 0)
    low, high = send(terms[half], 0, -1), send(terms[half + 1], 0, 1)
    low_a = send(jnp.concatenate([add(prev[:half], low_a), prev[half:]]), -1, 0)
    high_a = send(jnp.concatenate([succ[:half], add(succ[half:], high_a)]), 1, 0)
    for s in range(half - 1, 0, -1):
        low = send(add(terms[s], low), 0, -1)
    for s in range(half + 2, nz):
        high = send(add(terms[s], high), 0, 1)
    line = [add(own[s], low_a[s], high_a[s]) for s in range(nz)]
    s6 = send(line[6], 0, 2)
    s34 = send(jnp.stack(line[3:5]), 0, -2)
    s5 = send(line[5], 0, 2)
    s1 = send(add(line[1], s34[0]), 0, -1)
    s2 = send(add(line[2], s34[1]), 0, -2)
    s7 = send(add(line[7], s5), 0, 1)
    sum_a = add(line[0], s1, s2, s6, s7)
    line_b = [add(terms[0][s], low[s], high[s]) for s in range(NX)]
    sum_b = add(line_b[0], *[send(line_b[s], -s, 0) for s in range(1, NX)])
    first_key = jnp.concatenate([sum_a[:BLOCK], sum_b[:BLOCK]], axis=1)
    first_value = jnp.concatenate([sum_a[BLOCK:], sum_b[BLOCK:]], axis=1)
    key_grad = lax.dynamic_update_slice(key_grad, first_key, (0, 0))
    value_grad = lax.dynamic_update_slice(value_grad, first_value, (0, 0))
    return (key_grad, value_grad, hidden_grad)


def solution(mesh):
    in_specs = (
        P("dp", "tensor"),
        P("dp", "tensor"),
        P("dp", "tensor"),
        P("dp", "tensor"),
        P(None, "tensor"),
        P("dp"),
        P("dp"),
    )
    out_specs = (P("dp", "tensor"), P("dp", "tensor"), P("tensor", "dp"))
    return jax.shard_map(
        functools.partial(local, dp=mesh.shape["dp"]),
        mesh=mesh,
        in_specs=in_specs,
        out_specs=out_specs,
        check_vma=False,
    )
```

profile of v0, /device:TPU:16, one launch (start us, length us, event | category | flops | bytes accessed | tf_op | source)
XLA Modules:
  0.0 156.4 jit_solution(3138176209793748593)
XLA Ops:
  7.2 1.6 pack.1
  8.8 2.8 %collective-permute-start.12 = (bf16[256,128]{1,0:T(8,128)(2,1)}, bf16[256,128]{1,0:T(8,128)(2,1)S(1)}, u32[]{:S(2)}, u32[]{:S(2)}) collective-permute-start(bf16[256,128]{1,0:T(8,128)(2,1)} %get-tuple-element.22), channel_id=1, source_target_pairs={{0,192},{8,200},{16,208},{24,216},{32,224},{40,232},{48,240},{56,2... | collective-permute-start | bytes 196616 | tf_op jit(solution)/shard_map/ppermute | solution.py:187
  11.5 0.8 collective-permute-start.11
  12.3 0.9 collective-permute-start.10
  13.2 6.3 %collective-permute-start.5 = (bf16[272,128]{1,0:T(8,128)(2,1)}, bf16[272,128]{1,0:T(8,128)(2,1)S(1)}, u32[]{:S(2)}, u32[]{:S(2)}) collective-permute-start(bf16[272,128]{1,0:T(8,128)(2,1)} %get-tuple-element.21), channel_id=1, source_target_pairs={{0,48},{8,56},{16,0},{24,8},{32,16},{40,24},{48,32},{56,40},{64,11... | collective-permute-start | bytes 208904 | tf_op jit(solution)/shard_map/ppermute | solution.py:187
  19.5 1.0 collective-permute-start.3
  20.5 0.9 bitcast_dynamic-update-slice_fusion.3
  21.5 1.5 collective-permute-start.1
  23.0 0.9 pad_maximum_fusion.2.refs_5_
  23.9 0.7 collective-permute-start.13
  24.6 4.9 %collective-permute-done.1 = bf16[272,128]{1,0:T(8,128)(2,1)S(1)} collective-permute-done((bf16[272,128]{1,0:T(8,128)(2,1)}, bf16[272,128]{1,0:T(8,128)(2,1)S(1)}, u32[]{:S(2)}, u32[]{:S(2)}) %collective-permute-start.1) | collective-permute-done | bytes 69664 | tf_op jit(solution)/shard_map/ppermute | solution.py:187
  29.6 1.2 collective-permute-done
  30.8 0.1 collective-permute-start.2
  30.9 4.1 %collective-permute-start.4 = (bf16[272,128]{1,0:T(8,128)(2,1)S(1)}, bf16[272,128]{1,0:T(8,128)(2,1)S(1)}, u32[]{:S(2)}, u32[]{:S(2)}) collective-permute-start(bf16[272,128]{1,0:T(8,128)(2,1)S(1)} %collective-permute-done.3), channel_id=1, source_target_pairs={{0,48},{8,56},{16,0},{24,8},{32,16},{40,24},{48,32},{56,40},{64,11... | collective-permute-start | bytes 208904 | tf_op jit(solution)/shard_map/ppermute | solution.py:187
  35.0 5.9 %collective-permute-done.2 = bf16[2,272,128]{2,1,0:T(8,128)(2,1)S(1)} collective-permute-done((bf16[2,272,128]{2,1,0:T(8,128)(2,1)S(1)}, bf16[2,272,128]{2,1,0:T(8,128)(2,1)S(1)}, u32[]{:S(2)}, u32[]{:S(2)}) %collective-permute-start.2) | collective-permute-done | bytes 139296 | tf_op jit(solution)/shard_map/ppermute | solution.py:187
  41.0 2.4 %collective-permute-start.7 = (bf16[8,272,128]{2,1,0:T(8,128)(2,1)S(1)}, bf16[8,272,128]{2,1,0:T(8,128)(2,1)S(1)}, u32[]{:S(2)}, u32[]{:S(2)}) collective-permute-start(bf16[8,272,128]{2,1,0:T(8,128)(2,1)S(1)} %bitcast_dynamic-update-slice_fusion.refs_0_), channel_id=1, source_target_pairs={{0,192},{8,200},{16,208},{24,216},{32,224},{40,232},{48,240},{56,2... | collective-permute-start | bytes 1671176 | tf_op jit(solution)/shard_map/ppermute | solution.py:187
  43.5 2.0 %collective-permute-start.14 = (bf16[4,256,128]{2,1,0:T(8,128)(2,1)S(1)}, bf16[4,256,128]{2,1,0:T(8,128)(2,1)S(1)}, u32[]{:S(2)}, u32[]{:S(2)}) collective-permute-start(bf16[4,256,128]{2,1,0:T(8,128)(2,1)S(1)} %collective-permute-done.13.refs_6_), channel_id=1, source_target_pairs={{0,8},{8,16},{16,24},{24,32},{32,40},{40,48},{48,56},{56,0},{64,72... | collective-permute-start | bytes 786440 | tf_op jit(solution)/shard_map/ppermute | solution.py:187
  45.5 6.3 %collective-permute-done.17.refs_12_ = bf16[4,256,128]{2,1,0:T(8,128)(2,1)S(1)} collective-permute-done((bf16[4,256,128]{2,1,0:T(8,128)(2,1)S(1)}, bf16[4,256,128]{2,1,0:T(8,128)(2,1)S(1)}, u32[]{:S(2)}, u32[]{:S(2)}) %collective-permute-start.17) | collective-permute-done | bytes 262176 | tf_op jit(solution)/shard_map/ppermute | solution.py:187
  51.8 0.3 collective-permute-done.14.refs_7_
  52.1 2.1 %collective-permute-start.15 = (bf16[4,256,128]{2,1,0:T(8,128)(2,1)S(1)}, bf16[4,256,128]{2,1,0:T(8,128)(2,1)}, u32[]{:S(2)}, u32[]{:S(2)}) collective-permute-start(bf16[4,256,128]{2,1,0:T(8,128)(2,1)S(1)} %collective-permute-done.14.refs_7_), channel_id=1, source_target_pairs={{0,8},{8,16},{16,24},{24,32},{32,40},{40,48},{48,56},{56,0},{64,72... | collective-permute-start | bytes 786440 | tf_op jit(solution)/shard_map/ppermute | solution.py:187
  54.2 3.5 %collective-permute-start.9 = (bf16[4,272,128]{2,1,0:T(8,128)(2,1)S(1)}, bf16[4,272,128]{2,1,0:T(8,128)(2,1)S(1)}, u32[]{:S(2)}, u32[]{:S(2)}) collective-permute-start(bf16[4,272,128]{2,1,0:T(8,128)(2,1)S(1)} %slice.193), channel_id=1, source_target_pairs={{0,192},{8,200},{16,208},{24,216},{32,224},{40,232},{48,240},{56,2... | collective-permute-start | bytes 835592 | tf_op jit(solution)/shard_map/ppermute | solution.py:187
  57.7 0.1 collective-permute-start.8
  57.8 3.1 %collective-permute-done.18.refs_11_ = bf16[4,256,128]{2,1,0:T(8,128)(2,1)} collective-permute-done((bf16[4,256,128]{2,1,0:T(8,128)(2,1)S(1)}, bf16[4,256,128]{2,1,0:T(8,128)(2,1)}, u32[]{:S(2)}, u32[]{:S(2)}) %collective-permute-start.18) | collective-permute-done | bytes 262176 | tf_op jit(solution)/shard_map/ppermute | solution.py:187
  60.9 0.4 collective-permute-done.15.refs_8_
  61.4 1.9 %collective-permute-start.16 = (bf16[4,256,128]{2,1,0:T(8,128)(2,1)}, bf16[4,256,128]{2,1,0:T(8,128)(2,1)}, u32[]{:S(2)}, u32[]{:S(2)}) collective-permute-start(bf16[4,256,128]{2,1,0:T(8,128)(2,1)} %collective-permute-done.15.refs_8_), channel_id=1, source_target_pairs={{0,8},{8,16},{16,24},{24,32},{32,40},{40,48},{48,56},{56,0},{64,72... | collective-permute-start | bytes 786440 | tf_op jit(solution)/shard_map/ppermute | solution.py:187
  63.3 0.6 pad_add_fusion.spot
  63.9 3.7 %collective-permute-done.19.refs_10_ = bf16[4,256,128]{2,1,0:T(8,128)(2,1)} collective-permute-done((bf16[4,256,128]{2,1,0:T(8,128)(2,1)}, bf16[4,256,128]{2,1,0:T(8,128)(2,1)}, u32[]{:S(2)}, u32[]{:S(2)}) %collective-permute-start.19) | collective-permute-done | bytes 262176 | tf_op jit(solution)/shard_map/ppermute | solution.py:187
  67.6 1.6 %collective-permute-done.16.refs_9_ = bf16[4,256,128]{2,1,0:T(8,128)(2,1)} collective-permute-done((bf16[4,256,128]{2,1,0:T(8,128)(2,1)}, bf16[4,256,128]{2,1,0:T(8,128)(2,1)}, u32[]{:S(2)}, u32[]{:S(2)}) %collective-permute-start.16) | collective-permute-done | bytes 262176 | tf_op jit(solution)/shard_map/ppermute | solution.py:187
  69.3 24.8 %attention.1 = (bf16[768,256]{1,0:T(8,128)(2,1)}, bf16[768,256]{1,0:T(8,128)(2,1)}, bf16[4608,768]{1,0:T(8,128)(2,1)}, bf16[8,256,128]{2,1,0:T(8,128)(2,1)}, bf1...) custom-call(s32[6]{0:T(128)} %parents.3, ...), custom_call_target="tpu_custom_call" | custom-call | tf_op jit(solution)/shard_map/attention/pallas_call | solution.py:230
  94.3 2.9 %collective-permute-start.22 = (bf16[4,256,128]{2,1,0:T(8,128)(2,1)}, bf16[4,256,128]{2,1,0:T(8,128)(2,1)S(1)}, u32[]{:S(2)}, u32[]{:S(2)}) collective-permute-start(bf16[4,256,128]{2,1,0:T(8,128)(2,1)} %get-tuple-element.28), channel_id=1, source_target_pairs={{0,64},{8,72},{16,80},{24,88},{32,96},{40,104},{48,112},{56,120},{... | collective-permute-start | bytes 786440 | tf_op jit(solution)/shard_map/ppermute | solution.py:187
  97.3 2.3 %collective-permute-start.20 = (bf16[4,256,128]{2,1,0:T(8,128)(2,1)}, bf16[4,256,128]{2,1,0:T(8,128)(2,1)S(1)}, u32[]{:S(2)}, u32[]{:S(2)}) collective-permute-start(bf16[4,256,128]{2,1,0:T(8,128)(2,1)} %get-tuple-element.26), channel_id=1, source_target_pairs={{0,192},{8,200},{16,208},{24,216},{32,224},{40,232},{48,240},{56,2... | collective-permute-start | bytes 786440 | tf_op jit(solution)/shard_map/ppermute | solution.py:187
  99.6 0.2 collective-permute-start.30
  99.8 1.8 %collective-permute-start.34 = (bf16[4,256,128]{2,1,0:T(8,128)(2,1)S(1)}, bf16[4,256,128]{2,1,0:T(8,128)(2,1)S(1)}, u32[]{:S(2)}, u32[]{:S(2)}) collective-permute-start(bf16[4,256,128]{2,1,0:T(8,128)(2,1)S(1)} %copy-done.18), channel_id=1, source_target_pairs={{0,8},{8,16},{16,24},{24,32},{32,40},{40,48},{48,56},{56,0},{64,72... | collective-permute-start | bytes 786440 | tf_op jit(solution)/shard_map/ppermute | solution.py:187
  101.6 4.3 %collective-permute-done.22 = bf16[4,256,128]{2,1,0:T(8,128)(2,1)S(1)} collective-permute-done((bf16[4,256,128]{2,1,0:T(8,128)(2,1)}, bf16[4,256,128]{2,1,0:T(8,128)(2,1)S(1)}, u32[]{:S(2)}, u32[]{:S(2)}) %collective-permute-start.22) | collective-permute-done | bytes 262176 | tf_op jit(solution)/shard_map/ppermute | solution.py:187
  106.1 0.4 collective-permute-start.23
  106.5 0.3 collective-permute-done.20
  106.9 3.6 %collective-permute-start.21 = (bf16[8,256,128]{2,1,0:T(8,128)(2,1)S(1)}, bf16[8,256,128]{2,1,0:T(8,128)(2,1)S(1)}, u32[]{:S(2)}, u32[]{:S(2)}) collective-permute-start(bf16[8,256,128]{2,1,0:T(8,128)(2,1)S(1)} %pad_maximum_fusion), channel_id=1, source_target_pairs={{0,192},{8,200},{16,208},{24,216},{32,224},{40,232},{48,240},{56,2... | collective-permute-start | bytes 1572872 | tf_op jit(solution)/shard_map/ppermute | solution.py:187
  110.6 0.3 collective-permute-start.31
  110.9 2.1 %collective-permute-start.35 = (bf16[4,256,128]{2,1,0:T(8,128)(2,1)S(1)}, bf16[4,256,128]{2,1,0:T(8,128)(2,1)S(1)}, u32[]{:S(2)}, u32[]{:S(2)}) collective-permute-start(bf16[4,256,128]{2,1,0:T(8,128)(2,1)S(1)} %add_convert_fusion.1), channel_id=1, source_target_pairs={{0,8},{8,16},{16,24},{24,32},{32,40},{40,48},{48,56},{56,0},{64,72... | collective-permute-start | bytes 786440 | tf_op jit(solution)/shard_map/ppermute | solution.py:187
  113.0 4.2 %collective-permute-done.31 = bf16[4,256,128]{2,1,0:T(8,128)(2,1)S(1)} collective-permute-done((bf16[4,256,128]{2,1,0:T(8,128)(2,1)S(1)}, bf16[4,256,128]{2,1,0:T(8,128)(2,1)S(1)}, u32[]{:S(2)}, u32[]{:S(2)}) %collective-permute-start.31) | collective-permute-done | bytes 262176 | tf_op jit(solution)/shard_map/ppermute | solution.py:187
  117.3 0.1 add_convert_fusion.3
  117.4 2.9 %collective-permute-start.32 = (bf16[4,256,128]{2,1,0:T(8,128)(2,1)S(1)}, bf16[4,256,128]{2,1,0:T(8,128)(2,1)S(1)}, u32[]{:S(2)}, u32[]{:S(2)}) collective-permute-start(bf16[4,256,128]{2,1,0:T(8,128)(2,1)S(1)} %add_convert_fusion.3), channel_id=1, source_target_pairs={{0,56},{8,0},{16,8},{24,16},{32,24},{40,32},{48,40},{56,48},{64,12... | collective-permute-start | bytes 786440 | tf_op jit(solution)/shard_map/ppermute | solution.py:187
  120.4 0.1 collective-permute-start.24
  120.5 0.1 add_convert_fusion
  120.5 1.5 collective-permute-start.36
  122.1 9.1 %collective-permute-done.24 = bf16[2,256,128]{2,1,0:T(8,128)(2,1)S(1)} collective-permute-done((bf16[2,256,128]{2,1,0:T(8,128)(2,1)S(1)}, bf16[2,256,128]{2,1,0:T(8,128)(2,1)S(1)}, u32[]{:S(2)}, u32[]{:S(2)}) %collective-permute-start.24) | collective-permute-done | bytes 131104 | tf_op jit(solution)/shard_map/ppermute | solution.py:187
  131.2 0.1 fusion.16
  131.3 2.9 %collective-permute-start.28 = (bf16[256,128]{1,0:T(8,128)(2,1)S(1)}, bf16[256,128]{1,0:T(8,128)(2,1)S(1)}, u32[]{:S(2)}, u32[]{:S(2)}) collective-permute-start(bf16[256,128]{1,0:T(8,128)(2,1)S(1)} %get-tuple-element.41), channel_id=1, source_target_pairs={{0,16},{8,24},{16,32},{24,40},{32,48},{40,56},{48,0},{56,8},{64,80... | collective-permute-start | bytes 196616 | tf_op jit(solution)/shard_map/ppermute | solution.py:187
  134.3 0.1 collective-permute-start.33
  134.4 1.9 %collective-permute-start.25 = (bf16[256,128]{1,0:T(8,128)(2,1)S(1)}, bf16[256,128]{1,0:T(8,128)(2,1)S(1)}, u32[]{:S(2)}, u32[]{:S(2)}) collective-permute-start(bf16[256,128]{1,0:T(8,128)(2,1)S(1)} %get-tuple-element.39), channel_id=1, source_target_pairs={{0,56},{8,0},{16,8},{24,16},{32,24},{40,32},{48,40},{56,48},{64,12... | collective-permute-start | bytes 196616 | tf_op jit(solution)/shard_map/ppermute | solution.py:187
  136.3 2.4 %collective-permute-start.26 = (bf16[256,128]{1,0:T(8,128)(2,1)S(1)}, bf16[256,128]{1,0:T(8,128)(2,1)S(1)}, u32[]{:S(2)}, u32[]{:S(2)}) collective-permute-start(bf16[256,128]{1,0:T(8,128)(2,1)S(1)} %get-tuple-element.40), channel_id=1, source_target_pairs={{0,48},{8,56},{16,0},{24,8},{32,16},{40,24},{48,32},{56,40},{64,11... | collective-permute-start | bytes 196616 | tf_op jit(solution)/shard_map/ppermute | solution.py:187
  138.7 0.7 collective-permute-start.27
  139.5 0.1 collective-permute-start.29
  139.6 1.2 collective-permute-done.33
  140.8 0.1 fusion.13
  140.9 0.8 collective-permute-start.37
  141.7 0.1 collective-permute-done.25
  141.8 1.2 collective-permute-start.39
  143.0 0.7 collective-permute-start.38
  143.7 1.5 collective-permute-done.27
  145.2 0.5 collective-permute-done.29
  145.8 1.5 collective-permute-done.39
  147.3 1.5 collective-permute-done.38
  148.8 0.7 maximum_dynamic-update-slice_fusion
  (94 shorter events, 1.1 us)
Async XLA Ops:
  7.2 142.4 %reduce-scatter.2.cloned.1.call-start = ((), (), s32[]{:S(2)}) async-start(), calls=%async_computation.1 | async-start | bytes 7962624 | tf_op jit(solution)/shard_map/reduce_scatter | solution.py:277
  8.8 12.7 %collective-permute-start.12 = (bf16[256,128]{1,0:T(8,128)(2,1)}, bf16[256,128]{1,0:T(8,128)(2,1)S(1)}, u32[]{:S(2)}, u32[]{:S(2)}) collective-permute-start(bf16[256,128]{1,0:T(8,128)(2,1)} %get-tuple-element.22), channel_id=1, source_target_pairs={{0,192},{8,200},{16,208},{24,216},{32,224},{40,232},{48,240},{56,2... | collective-permute-start | bytes 196616 | tf_op jit(solution)/shard_map/ppermute | solution.py:187
  11.5 11.5 %collective-permute-start.11 = (bf16[256,128]{1,0:T(8,128)(2,1)}, bf16[256,128]{1,0:T(8,128)(2,1)S(1)}, u32[]{:S(2)}, u32[]{:S(2)}) collective-permute-start(bf16[256,128]{1,0:T(8,128)(2,1)} %get-tuple-element.22), channel_id=1, source_target_pairs={{0,128},{8,136},{16,144},{24,152},{32,160},{40,168},{48,176},{56,1... | collective-permute-start | bytes 196616 | tf_op jit(solution)/shard_map/ppermute | solution.py:187
  12.3 10.7 %collective-permute-start.10 = (bf16[256,128]{1,0:T(8,128)(2,1)}, bf16[256,128]{1,0:T(8,128)(2,1)S(1)}, u32[]{:S(2)}, u32[]{:S(2)}) collective-permute-start(bf16[256,128]{1,0:T(8,128)(2,1)} %get-tuple-element.22), channel_id=1, source_target_pairs={{0,64},{8,72},{16,80},{24,88},{32,96},{40,104},{48,112},{56,120},{... | collective-permute-start | bytes 196616 | tf_op jit(solution)/shard_map/ppermute | solution.py:187
  13.2 27.7 %collective-permute-start.5 = (bf16[272,128]{1,0:T(8,128)(2,1)}, bf16[272,128]{1,0:T(8,128)(2,1)S(1)}, u32[]{:S(2)}, u32[]{:S(2)}) collective-permute-start(bf16[272,128]{1,0:T(8,128)(2,1)} %get-tuple-element.21), channel_id=1, source_target_pairs={{0,48},{8,56},{16,0},{24,8},{32,16},{40,24},{48,32},{56,40},{64,11... | collective-permute-start | bytes 208904 | tf_op jit(solution)/shard_map/ppermute | solution.py:187
  19.5 11.4 %collective-permute-start.3 = (bf16[272,128]{1,0:T(8,128)(2,1)}, bf16[272,128]{1,0:T(8,128)(2,1)S(1)}, u32[]{:S(2)}, u32[]{:S(2)}) collective-permute-start(bf16[272,128]{1,0:T(8,128)(2,1)} %get-tuple-element.21), channel_id=1, source_target_pairs={{0,56},{8,0},{16,8},{24,16},{32,24},{40,32},{48,40},{56,48},{64,12... | collective-permute-start | bytes 208904 | tf_op jit(solution)/shard_map/ppermute | solution.py:187
  21.5 8.1 %collective-permute-start.1 = (bf16[272,128]{1,0:T(8,128)(2,1)}, bf16[272,128]{1,0:T(8,128)(2,1)S(1)}, u32[]{:S(2)}, u32[]{:S(2)}) collective-permute-start(bf16[272,128]{1,0:T(8,128)(2,1)} %get-tuple-element.21), channel_id=1, source_target_pairs={{0,16},{8,24},{16,32},{24,40},{32,48},{40,56},{48,0},{56,8},{64,80... | collective-permute-start | bytes 208904 | tf_op jit(solution)/shard_map/ppermute | solution.py:187
  23.0 7.8 %collective-permute-start = (bf16[272,128]{1,0:T(8,128)(2,1)}, bf16[272,128]{1,0:T(8,128)(2,1)S(1)}, u32[]{:S(2)}, u32[]{:S(2)}) collective-permute-start(bf16[272,128]{1,0:T(8,128)(2,1)} %get-tuple-element.21), channel_id=1, source_target_pairs={{0,8},{8,16},{16,24},{24,32},{32,40},{40,48},{48,56},{56,0},{64,72... | collective-permute-start | bytes 208904 | tf_op jit(solution)/shard_map/ppermute | solution.py:187
  23.9 45.4 %copy-start.2 = (bf16[4,256,128]{2,1,0:T(8,128)(2,1)}, bf16[4,256,128]{2,1,0:T(8,128)(2,1)S(1)}, u32[]{:S(2)}) copy-start(bf16[4,256,128]{2,1,0:T(8,128)(2,1)S(1)} %pad_maximum_fusion.2.refs_5_) | copy-start | bytes 786436
  23.9 19.5 %collective-permute-start.13 = (bf16[4,256,128]{2,1,0:T(8,128)(2,1)S(1)}, bf16[4,256,128]{2,1,0:T(8,128)(2,1)S(1)}, u32[]{:S(2)}, u32[]{:S(2)}) collective-permute-start(bf16[4,256,128]{2,1,0:T(8,128)(2,1)S(1)} %pad_maximum_fusion.2.refs_5_), channel_id=1, source_target_pairs={{0,8},{8,16},{16,24},{24,32},{32,40},{40,48},{48,56},{56,0},{64,72... | collective-permute-start | bytes 786440 | tf_op jit(solution)/shard_map/ppermute | solution.py:187
  30.8 10.1 %collective-permute-start.2 = (bf16[2,272,128]{2,1,0:T(8,128)(2,1)S(1)}, bf16[2,272,128]{2,1,0:T(8,128)(2,1)S(1)}, u32[]{:S(2)}, u32[]{:S(2)}) collective-permute-start(bf16[2,272,128]{2,1,0:T(8,128)(2,1)S(1)} %pad_maximum_fusion.3), channel_id=1, source_target_pairs={{0,16},{8,24},{16,32},{24,40},{32,48},{40,56},{48,0},{56,8},{64,80... | collective-permute-start | bytes 417800 | tf_op jit(solution)/shard_map/ppermute | solution.py:187
  30.9 10.0 %collective-permute-start.4 = (bf16[272,128]{1,0:T(8,128)(2,1)S(1)}, bf16[272,128]{1,0:T(8,128)(2,1)S(1)}, u32[]{:S(2)}, u32[]{:S(2)}) collective-permute-start(bf16[272,128]{1,0:T(8,128)(2,1)S(1)} %collective-permute-done.3), channel_id=1, source_target_pairs={{0,48},{8,56},{16,0},{24,8},{32,16},{40,24},{48,32},{56,40},{64,11... | collective-permute-start | bytes 208904 | tf_op jit(solution)/shard_map/ppermute | solution.py:187
  41.0 28.3 %copy-start.3 = (bf16[8,272,128]{2,1,0:T(8,128)(2,1)}, bf16[8,272,128]{2,1,0:T(8,128)(2,1)S(1)}, u32[]{:S(2)}) copy-start(bf16[8,272,128]{2,1,0:T(8,128)(2,1)S(1)} %bitcast_dynamic-update-slice_fusion.refs_0_) | copy-start | bytes 1671172
  41.0 13.2 %collective-permute-start.7 = (bf16[8,272,128]{2,1,0:T(8,128)(2,1)S(1)}, bf16[8,272,128]{2,1,0:T(8,128)(2,1)S(1)}, u32[]{:S(2)}, u32[]{:S(2)}) collective-permute-start(bf16[8,272,128]{2,1,0:T(8,128)(2,1)S(1)} %bitcast_dynamic-update-slice_fusion.refs_0_), channel_id=1, source_target_pairs={{0,192},{8,200},{16,208},{24,216},{32,224},{40,232},{48,240},{56,2... | collective-permute-start | bytes 1671176 | tf_op jit(solution)/shard_map/ppermute | solution.py:187
  43.4 14.3 %collective-permute-start.6 = (bf16[8,272,128]{2,1,0:T(8,128)(2,1)S(1)}, bf16[8,272,128]{2,1,0:T(8,128)(2,1)S(1)}, u32[]{:S(2)}, u32[]{:S(2)}) collective-permute-start(bf16[8,272,128]{2,1,0:T(8,128)(2,1)S(1)} %bitcast_dynamic-update-slice_fusion.refs_0_), channel_id=1, source_target_pairs={{0,64},{8,72},{16,80},{24,88},{32,96},{40,104},{48,112},{56,120},{... | collective-permute-start | bytes 1671176 | tf_op jit(solution)/shard_map/ppermute | solution.py:187
  43.4 8.4 %collective-permute-start.17 = (bf16[4,256,128]{2,1,0:T(8,128)(2,1)S(1)}, bf16[4,256,128]{2,1,0:T(8,128)(2,1)S(1)}, u32[]{:S(2)}, u32[]{:S(2)}) collective-permute-start(bf16[4,256,128]{2,1,0:T(8,128)(2,1)S(1)} %pad_maximum_fusion.2.refs_5_), channel_id=1, source_target_pairs={{0,56},{8,0},{16,8},{24,16},{32,24},{40,32},{48,40},{56,48},{64,12... | collective-permute-start | bytes 786440 | tf_op jit(solution)/shard_map/ppermute | solution.py:187
  43.4 25.8 %copy-start.9 = (bf16[4,256,128]{2,1,0:T(8,128)(2,1)}, bf16[4,256,128]{2,1,0:T(8,128)(2,1)S(1)}, u32[]{:S(2)}) copy-start(bf16[4,256,128]{2,1,0:T(8,128)(2,1)S(1)} %collective-permute-done.13.refs_6_) | copy-start | bytes 786436
  43.5 8.6 %collective-permute-start.14 = (bf16[4,256,128]{2,1,0:T(8,128)(2,1)S(1)}, bf16[4,256,128]{2,1,0:T(8,128)(2,1)S(1)}, u32[]{:S(2)}, u32[]{:S(2)}) collective-permute-start(bf16[4,256,128]{2,1,0:T(8,128)(2,1)S(1)} %collective-permute-done.13.refs_6_), channel_id=1, source_target_pairs={{0,8},{8,16},{16,24},{24,32},{32,40},{40,48},{48,56},{56,0},{64,72... | collective-permute-start | bytes 786440 | tf_op jit(solution)/shard_map/ppermute | solution.py:187
  51.8 6.0 %copy-start.11 = (bf16[4,256,128]{2,1,0:T(8,128)(2,1)}, bf16[4,256,128]{2,1,0:T(8,128)(2,1)S(1)}, u32[]{:S(2)}) copy-start(bf16[4,256,128]{2,1,0:T(8,128)(2,1)S(1)} %collective-permute-done.17.refs_12_) | copy-start | bytes 786436
  51.8 9.1 %collective-permute-start.18 = (bf16[4,256,128]{2,1,0:T(8,128)(2,1)S(1)}, bf16[4,256,128]{2,1,0:T(8,128)(2,1)}, u32[]{:S(2)}, u32[]{:S(2)}) collective-permute-start(bf16[4,256,128]{2,1,0:T(8,128)(2,1)S(1)} %collective-permute-done.17.refs_12_), channel_id=1, source_target_pairs={{0,56},{8,0},{16,8},{24,16},{32,24},{40,32},{48,40},{56,48},{64,12... | collective-permute-start | bytes 786440 | tf_op jit(solution)/shard_map/ppermute | solution.py:187
  52.1 8.8 %copy-start.12 = (bf16[4,256,128]{2,1,0:T(8,128)(2,1)}, bf16[4,256,128]{2,1,0:T(8,128)(2,1)S(1)}, u32[]{:S(2)}) copy-start(bf16[4,256,128]{2,1,0:T(8,128)(2,1)S(1)} %collective-permute-done.14.refs_7_) | copy-start | bytes 786436
  52.1 9.3 %collective-permute-start.15 = (bf16[4,256,128]{2,1,0:T(8,128)(2,1)S(1)}, bf16[4,256,128]{2,1,0:T(8,128)(2,1)}, u32[]{:S(2)}, u32[]{:S(2)}) collective-permute-start(bf16[4,256,128]{2,1,0:T(8,128)(2,1)S(1)} %collective-permute-done.14.refs_7_), channel_id=1, source_target_pairs={{0,8},{8,16},{16,24},{24,32},{32,40},{40,48},{48,56},{56,0},{64,72... | collective-permute-start | bytes 786440 | tf_op jit(solution)/shard_map/ppermute | solution.py:187
  54.2 15.1 %copy-start = (bf16[8,272,128]{2,1,0:T(8,128)(2,1)}, bf16[8,272,128]{2,1,0:T(8,128)(2,1)S(1)}, u32[]{:S(2)}) copy-start(bf16[8,272,128]{2,1,0:T(8,128)(2,1)S(1)} %collective-permute-done.7.refs_2_) | copy-start | bytes 1671172
  54.2 13.4 %collective-permute-start.9 = (bf16[4,272,128]{2,1,0:T(8,128)(2,1)S(1)}, bf16[4,272,128]{2,1,0:T(8,128)(2,1)S(1)}, u32[]{:S(2)}, u32[]{:S(2)}) collective-permute-start(bf16[4,272,128]{2,1,0:T(8,128)(2,1)S(1)} %slice.193), channel_id=1, source_target_pairs={{0,192},{8,200},{16,208},{24,216},{32,224},{40,232},{48,240},{56,2... | collective-permute-start | bytes 835592 | tf_op jit(solution)/shard_map/ppermute | solution.py:187
  57.7 11.6 %copy-start.1 = (bf16[8,272,128]{2,1,0:T(8,128)(2,1)}, bf16[8,272,128]{2,1,0:T(8,128)(2,1)S(1)}, u32[]{:S(2)}) copy-start(bf16[8,272,128]{2,1,0:T(8,128)(2,1)S(1)} %collective-permute-done.6.refs_1_) | copy-start | bytes 1671172
  57.7 9.9 %collective-permute-start.8 = (bf16[4,272,128]{2,1,0:T(8,128)(2,1)S(1)}, bf16[4,272,128]{2,1,0:T(8,128)(2,1)S(1)}, u32[]{:S(2)}, u32[]{:S(2)}) collective-permute-start(bf16[4,272,128]{2,1,0:T(8,128)(2,1)S(1)} %slice.192), channel_id=1, source_target_pairs={{0,64},{8,72},{16,80},{24,88},{32,96},{40,104},{48,112},{56,120},{... | collective-permute-start | bytes 835592 | tf_op jit(solution)/shard_map/ppermute | solution.py:187
  60.9 6.7 %collective-permute-start.19 = (bf16[4,256,128]{2,1,0:T(8,128)(2,1)}, bf16[4,256,128]{2,1,0:T(8,128)(2,1)}, u32[]{:S(2)}, u32[]{:S(2)}) collective-permute-start(bf16[4,256,128]{2,1,0:T(8,128)(2,1)} %collective-permute-done.18.refs_11_), channel_id=1, source_target_pairs={{0,56},{8,0},{16,8},{24,16},{32,24},{40,32},{48,40},{56,48},{64,12... | collective-permute-start | bytes 786440 | tf_op jit(solution)/shard_map/ppermute | solution.py:187
  61.4 7.9 %collective-permute-start.16 = (bf16[4,256,128]{2,1,0:T(8,128)(2,1)}, bf16[4,256,128]{2,1,0:T(8,128)(2,1)}, u32[]{:S(2)}, u32[]{:S(2)}) collective-permute-start(bf16[4,256,128]{2,1,0:T(8,128)(2,1)} %collective-permute-done.15.refs_8_), channel_id=1, source_target_pairs={{0,8},{8,16},{16,24},{24,32},{32,40},{40,48},{48,56},{56,0},{64,72... | collective-permute-start | bytes 786440 | tf_op jit(solution)/shard_map/ppermute | solution.py:187
  67.6 1.7 %copy-start.7 = (bf16[4,272,128]{2,1,0:T(8,128)(2,1)}, bf16[4,272,128]{2,1,0:T(8,128)(2,1)S(1)}, u32[]{:S(2)}) copy-start(bf16[4,272,128]{2,1,0:T(8,128)(2,1)S(1)} %collective-permute-done.9.refs_4_) | copy-start | bytes 835588
  67.6 1.7 %copy-start.8 = (bf16[4,272,128]{2,1,0:T(8,128)(2,1)}, bf16[4,272,128]{2,1,0:T(8,128)(2,1)S(1)}, u32[]{:S(2)}) copy-start(bf16[4,272,128]{2,1,0:T(8,128)(2,1)S(1)} %collective-permute-done.8.refs_3_) | copy-start | bytes 835588
  94.2 3.1 %copy-start.4 = (bf16[8,256,128]{2,1,0:T(8,128)(2,1)S(1)}, bf16[8,256,128]{2,1,0:T(8,128)(2,1)}, u32[]{:S(2)}) copy-start(bf16[8,256,128]{2,1,0:T(8,128)(2,1)} %get-tuple-element.25) | copy-start | bytes 1572868
  94.2 3.1 %copy-start.5 = (bf16[8,256,128]{2,1,0:T(8,128)(2,1)S(1)}, bf16[8,256,128]{2,1,0:T(8,128)(2,1)}, u32[]{:S(2)}) copy-start(bf16[8,256,128]{2,1,0:T(8,128)(2,1)} %get-tuple-element.27) | copy-start | bytes 1572868
  94.2 5.4 %copy-start.19 = (bf16[4,256,128]{2,1,0:T(8,128)(2,1)S(1)}, bf16[4,256,128]{2,1,0:T(8,128)(2,1)}, u32[]{:S(2)}) copy-start(bf16[4,256,128]{2,1,0:T(8,128)(2,1)} %get-tuple-element.33) | copy-start | bytes 786436
  94.2 5.6 %copy-start.18 = (bf16[4,256,128]{2,1,0:T(8,128)(2,1)S(1)}, bf16[4,256,128]{2,1,0:T(8,128)(2,1)}, u32[]{:S(2)}) copy-start(bf16[4,256,128]{2,1,0:T(8,128)(2,1)} %get-tuple-element.36) | copy-start | bytes 786436
  94.2 16.3 %copy-start.16 = (bf16[4,256,128]{2,1,0:T(8,128)(2,1)S(1)}, bf16[4,256,128]{2,1,0:T(8,128)(2,1)}, u32[]{:S(2)}) copy-start(bf16[4,256,128]{2,1,0:T(8,128)(2,1)} %get-tuple-element.32) | copy-start | bytes 786436
  94.2 16.6 %copy-start.15 = (bf16[4,256,128]{2,1,0:T(8,128)(2,1)S(1)}, bf16[4,256,128]{2,1,0:T(8,128)(2,1)}, u32[]{:S(2)}) copy-start(bf16[4,256,128]{2,1,0:T(8,128)(2,1)} %get-tuple-element.35) | copy-start | bytes 786436
  94.2 23.1 %copy-start.14 = (bf16[4,256,128]{2,1,0:T(8,128)(2,1)S(1)}, bf16[4,256,128]{2,1,0:T(8,128)(2,1)}, u32[]{:S(2)}) copy-start(bf16[4,256,128]{2,1,0:T(8,128)(2,1)} %get-tuple-element.31) | copy-start | bytes 786436
  94.2 26.0 %copy-start.6 = (bf16[8,256,128]{2,1,0:T(8,128)(2,1)S(1)}, bf16[8,256,128]{2,1,0:T(8,128)(2,1)}, u32[]{:S(2)}) copy-start(bf16[8,256,128]{2,1,0:T(8,128)(2,1)} %get-tuple-element.24) | copy-start | bytes 1572868
  94.2 26.2 %copy-start.13 = (bf16[4,256,128]{2,1,0:T(8,128)(2,1)S(1)}, bf16[4,256,128]{2,1,0:T(8,128)(2,1)}, u32[]{:S(2)}) copy-start(bf16[4,256,128]{2,1,0:T(8,128)(2,1)} %get-tuple-element.34) | copy-start | bytes 786436
  94.2 40.0 %copy-start.10 = (bf16[4,256,128]{2,1,0:T(8,128)(2,1)S(1)}, bf16[4,256,128]{2,1,0:T(8,128)(2,1)}, u32[]{:S(2)}) copy-start(bf16[4,256,128]{2,1,0:T(8,128)(2,1)} %get-tuple-element.30) | copy-start | bytes 786436
  94.3 46.5 %copy-start.17 = (bf16[4,256,128]{2,1,0:T(8,128)(2,1)S(1)}, bf16[4,256,128]{2,1,0:T(8,128)(2,1)}, u32[]{:S(2)}) copy-start(bf16[4,256,128]{2,1,0:T(8,128)(2,1)} %get-tuple-element.29) | copy-start | bytes 786436
  94.3 11.7 %collective-permute-start.22 = (bf16[4,256,128]{2,1,0:T(8,128)(2,1)}, bf16[4,256,128]{2,1,0:T(8,128)(2,1)S(1)}, u32[]{:S(2)}, u32[]{:S(2)}) collective-permute-start(bf16[4,256,128]{2,1,0:T(8,128)(2,1)} %get-tuple-element.28), channel_id=1, source_target_pairs={{0,64},{8,72},{16,80},{24,88},{32,96},{40,104},{48,112},{56,120},{... | collective-permute-start | bytes 786440 | tf_op jit(solution)/shard_map/ppermute | solution.py:187
  97.3 9.4 %collective-permute-start.20 = (bf16[4,256,128]{2,1,0:T(8,128)(2,1)}, bf16[4,256,128]{2,1,0:T(8,128)(2,1)S(1)}, u32[]{:S(2)}, u32[]{:S(2)}) collective-permute-start(bf16[4,256,128]{2,1,0:T(8,128)(2,1)} %get-tuple-element.26), channel_id=1, source_target_pairs={{0,192},{8,200},{16,208},{24,216},{32,224},{40,232},{48,240},{56,2... | collective-permute-start | bytes 786440 | tf_op jit(solution)/shard_map/ppermute | solution.py:187
  99.6 10.9 %collective-permute-start.30 = (bf16[4,256,128]{2,1,0:T(8,128)(2,1)S(1)}, bf16[4,256,128]{2,1,0:T(8,128)(2,1)S(1)}, u32[]{:S(2)}, u32[]{:S(2)}) collective-permute-start(bf16[4,256,128]{2,1,0:T(8,128)(2,1)S(1)} %copy-done.19), channel_id=1, source_target_pairs={{0,56},{8,0},{16,8},{24,16},{32,24},{40,32},{48,40},{56,48},{64,12... | collective-permute-start | bytes 786440 | tf_op jit(solution)/shard_map/ppermute | solution.py:187
  99.8 11.0 %collective-permute-start.34 = (bf16[4,256,128]{2,1,0:T(8,128)(2,1)S(1)}, bf16[4,256,128]{2,1,0:T(8,128)(2,1)S(1)}, u32[]{:S(2)}, u32[]{:S(2)}) collective-permute-start(bf16[4,256,128]{2,1,0:T(8,128)(2,1)S(1)} %copy-done.18), channel_id=1, source_target_pairs={{0,8},{8,16},{16,24},{24,32},{32,40},{40,48},{48,56},{56,0},{64,72... | collective-permute-start | bytes 786440 | tf_op jit(solution)/shard_map/ppermute | solution.py:187
  106.1 14.2 %collective-permute-start.23 = (bf16[8,256,128]{2,1,0:T(8,128)(2,1)S(1)}, bf16[8,256,128]{2,1,0:T(8,128)(2,1)S(1)}, u32[]{:S(2)}, u32[]{:S(2)}) collective-permute-start(bf16[8,256,128]{2,1,0:T(8,128)(2,1)S(1)} %pad_maximum_fusion.1), channel_id=1, source_target_pairs={{0,64},{8,72},{16,80},{24,88},{32,96},{40,104},{48,112},{56,120},{... | collective-permute-start | bytes 1572872 | tf_op jit(solution)/shard_map/ppermute | solution.py:187
  106.9 13.4 %collective-permute-start.21 = (bf16[8,256,128]{2,1,0:T(8,128)(2,1)S(1)}, bf16[8,256,128]{2,1,0:T(8,128)(2,1)S(1)}, u32[]{:S(2)}, u32[]{:S(2)}) collective-permute-start(bf16[8,256,128]{2,1,0:T(8,128)(2,1)S(1)} %pad_maximum_fusion), channel_id=1, source_target_pairs={{0,192},{8,200},{16,208},{24,216},{32,224},{40,232},{48,240},{56,2... | collective-permute-start | bytes 1572872 | tf_op jit(solution)/shard_map/ppermute | solution.py:187
  110.6 6.7 %collective-permute-start.31 = (bf16[4,256,128]{2,1,0:T(8,128)(2,1)S(1)}, bf16[4,256,128]{2,1,0:T(8,128)(2,1)S(1)}, u32[]{:S(2)}, u32[]{:S(2)}) collective-permute-start(bf16[4,256,128]{2,1,0:T(8,128)(2,1)S(1)} %add_convert_fusion.4), channel_id=1, source_target_pairs={{0,56},{8,0},{16,8},{24,16},{32,24},{40,32},{48,40},{56,48},{64,12... | collective-permute-start | bytes 786440 | tf_op jit(solution)/shard_map/ppermute | solution.py:187
  110.9 9.6 %collective-permute-start.35 = (bf16[4,256,128]{2,1,0:T(8,128)(2,1)S(1)}, bf16[4,256,128]{2,1,0:T(8,128)(2,1)S(1)}, u32[]{:S(2)}, u32[]{:S(2)}) collective-permute-start(bf16[4,256,128]{2,1,0:T(8,128)(2,1)S(1)} %add_convert_fusion.1), channel_id=1, source_target_pairs={{0,8},{8,16},{16,24},{24,32},{32,40},{40,48},{48,56},{56,0},{64,72... | collective-permute-start | bytes 786440 | tf_op jit(solution)/shard_map/ppermute | solution.py:187
  117.4 16.9 %collective-permute-start.32 = (bf16[4,256,128]{2,1,0:T(8,128)(2,1)S(1)}, bf16[4,256,128]{2,1,0:T(8,128)(2,1)S(1)}, u32[]{:S(2)}, u32[]{:S(2)}) collective-permute-start(bf16[4,256,128]{2,1,0:T(8,128)(2,1)S(1)} %add_convert_fusion.3), channel_id=1, source_target_pairs={{0,56},{8,0},{16,8},{24,16},{32,24},{40,32},{48,40},{56,48},{64,12... | collective-permute-start | bytes 786440 | tf_op jit(solution)/shard_map/ppermute | solution.py:187
  120.4 10.9 %collective-permute-start.24 = (bf16[2,256,128]{2,1,0:T(8,128)(2,1)S(1)}, bf16[2,256,128]{2,1,0:T(8,128)(2,1)S(1)}, u32[]{:S(2)}, u32[]{:S(2)}) collective-permute-start(bf16[2,256,128]{2,1,0:T(8,128)(2,1)S(1)} %pad_maximum_fusion.4), channel_id=1, source_target_pairs={{0,48},{8,56},{16,0},{24,8},{32,16},{40,24},{48,32},{56,40},{64,11... | collective-permute-start | bytes 393224 | tf_op jit(solution)/shard_map/ppermute | solution.py:187
  120.5 18.9 %collective-permute-start.36 = (bf16[4,256,128]{2,1,0:T(8,128)(2,1)S(1)}, bf16[4,256,128]{2,1,0:T(8,128)(2,1)S(1)}, u32[]{:S(2)}, u32[]{:S(2)}) collective-permute-start(bf16[4,256,128]{2,1,0:T(8,128)(2,1)S(1)} %add_convert_fusion), channel_id=1, source_target_pairs={{0,8},{8,16},{16,24},{24,32},{32,40},{40,48},{48,56},{56,0},{64,72... | collective-permute-start | bytes 786440 | tf_op jit(solution)/shard_map/ppermute | solution.py:187
  131.3 7.4 %collective-permute-start.28 = (bf16[256,128]{1,0:T(8,128)(2,1)S(1)}, bf16[256,128]{1,0:T(8,128)(2,1)S(1)}, u32[]{:S(2)}, u32[]{:S(2)}) collective-permute-start(bf16[256,128]{1,0:T(8,128)(2,1)S(1)} %get-tuple-element.41), channel_id=1, source_target_pairs={{0,16},{8,24},{16,32},{24,40},{32,48},{40,56},{48,0},{56,8},{64,80... | collective-permute-start | bytes 196616 | tf_op jit(solution)/shard_map/ppermute | solution.py:187
  134.3 6.5 %collective-permute-start.33 = (bf16[4,256,128]{2,1,0:T(8,128)(2,1)S(1)}, bf16[4,256,128]{2,1,0:T(8,128)(2,1)S(1)}, u32[]{:S(2)}, u32[]{:S(2)}) collective-permute-start(bf16[4,256,128]{2,1,0:T(8,128)(2,1)S(1)} %add_convert_fusion.2), channel_id=1, source_target_pairs={{0,56},{8,0},{16,8},{24,16},{32,24},{40,32},{48,40},{56,48},{64,12... | collective-permute-start | bytes 786440 | tf_op jit(solution)/shard_map/ppermute | solution.py:187
  134.4 7.4 %collective-permute-start.25 = (bf16[256,128]{1,0:T(8,128)(2,1)S(1)}, bf16[256,128]{1,0:T(8,128)(2,1)S(1)}, u32[]{:S(2)}, u32[]{:S(2)}) collective-permute-start(bf16[256,128]{1,0:T(8,128)(2,1)S(1)} %get-tuple-element.39), channel_id=1, source_target_pairs={{0,56},{8,0},{16,8},{24,16},{32,24},{40,32},{48,40},{56,48},{64,12... | collective-permute-start | bytes 196616 | tf_op jit(solution)/shard_map/ppermute | solution.py:187
  136.3 6.7 %collective-permute-start.26 = (bf16[256,128]{1,0:T(8,128)(2,1)S(1)}, bf16[256,128]{1,0:T(8,128)(2,1)S(1)}, u32[]{:S(2)}, u32[]{:S(2)}) collective-permute-start(bf16[256,128]{1,0:T(8,128)(2,1)S(1)} %get-tuple-element.40), channel_id=1, source_target_pairs={{0,48},{8,56},{16,0},{24,8},{32,16},{40,24},{48,32},{56,40},{64,11... | collective-permute-start | bytes 196616 | tf_op jit(solution)/shard_map/ppermute | solution.py:187
  138.7 6.5 %collective-permute-start.27 = (bf16[256,128]{1,0:T(8,128)(2,1)S(1)}, bf16[256,128]{1,0:T(8,128)(2,1)S(1)}, u32[]{:S(2)}, u32[]{:S(2)}) collective-permute-start(bf16[256,128]{1,0:T(8,128)(2,1)S(1)} %get-tuple-element.42), channel_id=1, source_target_pairs={{0,16},{8,24},{16,32},{24,40},{32,48},{40,56},{48,0},{56,8},{64,80... | collective-permute-start | bytes 196616 | tf_op jit(solution)/shard_map/ppermute | solution.py:187
  139.5 6.3 %collective-permute-start.29 = (bf16[256,128]{1,0:T(8,128)(2,1)S(1)}, bf16[256,128]{1,0:T(8,128)(2,1)S(1)}, u32[]{:S(2)}, u32[]{:S(2)}) collective-permute-start(bf16[256,128]{1,0:T(8,128)(2,1)S(1)} %fusion.3), channel_id=1, source_target_pairs={{0,8},{8,16},{16,24},{24,32},{32,40},{40,48},{48,56},{56,0},{64,72... | collective-permute-start | bytes 196616 | tf_op jit(solution)/shard_map/ppermute | solution.py:187
  140.9 4.9 %collective-permute-start.37 = (bf16[256,128]{1,0:T(8,128)(2,1)S(1)}, bf16[256,128]{1,0:T(8,128)(2,1)S(1)}, u32[]{:S(2)}, u32[]{:S(2)}) collective-permute-start(bf16[256,128]{1,0:T(8,128)(2,1)S(1)} %get-tuple-element.45), channel_id=1, source_target_pairs={{0,192},{8,200},{16,208},{24,216},{32,224},{40,232},{48,240},{56,2... | collective-permute-start | bytes 196616 | tf_op jit(solution)/shard_map/ppermute | solution.py:187
  141.8 5.5 %collective-permute-start.39 = (bf16[256,128]{1,0:T(8,128)(2,1)S(1)}, bf16[256,128]{1,0:T(8,128)(2,1)S(1)}, u32[]{:S(2)}, u32[]{:S(2)}) collective-permute-start(bf16[256,128]{1,0:T(8,128)(2,1)S(1)} %get-tuple-element.46), channel_id=1, source_target_pairs={{0,64},{8,72},{16,80},{24,88},{32,96},{40,104},{48,112},{56,120},{... | collective-permute-start | bytes 196616 | tf_op jit(solution)/shard_map/ppermute | solution.py:187
  143.0 5.8 %collective-permute-start.38 = (bf16[256,128]{1,0:T(8,128)(2,1)S(1)}, bf16[256,128]{1,0:T(8,128)(2,1)S(1)}, u32[]{:S(2)}, u32[]{:S(2)}) collective-permute-start(bf16[256,128]{1,0:T(8,128)(2,1)S(1)} %get-tuple-element.47), channel_id=1, source_target_pairs={{0,128},{8,136},{16,144},{24,152},{32,160},{40,168},{48,176},{56,1... | collective-permute-start | bytes 196616 | tf_op jit(solution)/shard_map/ppermute | solution.py:187
Sparse Core Ops, SparseCore 0:
  94.4 43.8 reduce-scatter.1
where the time goes:
time: 157 us; the launch traced here: 156 us
  starting transfers between devices  59.3 us (38%)
  waiting for transfers between devices  51.8 us (33%)
  Pallas kernels  26.4 us (17%)
  between operations  14.5 us (9%)
  other arithmetic  3.22 us (2%)
    ppermute x40, starting transfers between devices, send(): return lax.ppermute(array, 'dp', pairs)  59.2 us
    ppermute x40, waiting for transfers between devices, send(): return lax.ppermute(array, 'dp', pairs)  51.8 us
    pallas_call x1, Pallas kernels, local(): pl.pallas_call(functools.partial(main_kernel, node_count, nz), grid=(node...  24.8 us
  transfers between devices with their start and end apart: 41, of which 19 were waited for; matrix products, arithmetic and copies ran while one was open for 3% of the time, Pallas kernels for 0%

commit v1 on v0

--- a/solution.py
+++ b/solution.py
@@ -12,6 +12,8 @@
 BLOCK = 128
 QSCALAR = 144
 META = 16
+TILES = 6
+UNROLL = 1
 NX = 4
 F32, BF16 = jnp.float32, jnp.bfloat16
 
@@ -32,64 +34,88 @@
     a_ref[2 * BLOCK :] = meta.astype(F32).astype(BF16)
 
 
-def main_kernel(node_count, nz, parents, lengths, spot, q_ref, k_ref, v_ref, g_ref, w_ref, *refs):
+def main_kernel(node_count, nz, parents, lengths, spot, q_hbm, k_hbm, v_hbm, g_hbm, w_hbm, *refs):
     parts, refs = refs[: 5 + nz], refs[5 + nz :]
-    kg_ref, vg_ref, out_ref = refs[:3]
+    kg_hbm, vg_hbm, out_hbm = refs[:3]
     terms, refs = refs[3 : 8 + nz], refs[8 + nz :]
-    far_a, far_b, acc_a, acc_b, send_a, send_b, qg_ref, meta_v, meta_s, sem, out_sem, meta_sem = refs
+    q_ref, k_ref, v_ref, g_ref, w_ref, kg_ref, vg_ref, qg_ref, out_ref, *refs = refs
+    far_a, far_b, acc_a, acc_b, send_a, send_b, meta_v, meta_s, *sems = refs
+    own_sem, far_sem, term_sem, grad_sem, out_sem, one_sem = sems
     half = nz // 2
-    step = pl.program_id(0)
     pieces = [(0, nz), (nz, nz), (3 * nz, nz), (2 * nz, half), (2 * nz + half, half)]
     ranges = [(0, at, size) for at, size in pieces] + [(1, sz * NX, NX) for sz in range(nz)]
-
-    def copies_in():
-        return [
-            pltpu.make_async_copy(part, (far_a, far_b)[h].at[pl.ds(at, size)], sem.at[i])
-            for i, (part, (h, at, size)) in enumerate(zip(parts, ranges))
-        ]
-
-    def copies_out():
-        return [
-            pltpu.make_async_copy((send_a, send_b)[h].at[pl.ds(at, size)], term, out_sem.at[i])
-            for i, (term, (h, at, size)) in enumerate(zip(terms, ranges))
-        ]
-
-    @pl.when(step == 0)
-    def _():
-        for copy in copies_in():
-            copy.start()
-        acc_a[...] = jnp.zeros_like(acc_a)
-        acc_b[...] = jnp.zeros_like(acc_b)
-        for copy in copies_in():
-            copy.wait()
-        meta = jnp.max(far_a[:, 2 * BLOCK :, :].astype(F32), axis=1)
-        meta_v[...] = meta.astype(jnp.int32)
-        copy = pltpu.make_async_copy(meta_v, meta_s, meta_sem)
+    own_pairs = [(q_hbm, q_ref), (k_hbm, k_ref), (v_hbm, v_ref), (g_hbm, g_ref)]
+    own_copies = [pltpu.make_async_copy(a, b, own_sem.at[i]) for i, (a, b) in enumerate(own_pairs)]
+    far_copies = [
+        pltpu.make_async_copy(part, (far_a, far_b)[h].at[pl.ds(at, size)], far_sem.at[i])
+        for i, (part, (h, at, size)) in enumerate(zip(parts, ranges))
+    ]
+    term_copies = [
+        pltpu.make_async_copy((send_a, send_b)[h].at[pl.ds(at, size)], term, term_sem.at[i])
+        for i, (term, (h, at, size)) in enumerate(zip(terms, ranges))
+    ]
+    grad_copies = [
+        pltpu.make_async_copy(kg_ref, kg_hbm, grad_sem.at[0]),
+        pltpu.make_async_copy(vg_ref, vg_hbm, grad_sem.at[1]),
+    ]
+    weight_copy = pltpu.make_async_copy(w_hbm, w_ref, one_sem.at[0])
+    meta_copy = pltpu.make_async_copy(meta_v, meta_s, one_sem.at[1])
+
+    for copy in far_copies + own_copies + [weight_copy]:
         copy.start()
+
+    def clear(i, carry):
+        acc_a[i] = jnp.zeros((2 * BLOCK, HEAD), F32)
+        acc_b[i] = jnp.zeros((2 * BLOCK, HEAD), F32)
+        return carry
+
+    lax.fori_loop(0, NX * nz + 1, clear, 0)
+    for copy in far_copies:
         copy.wait()
-
-    @pl.when(step < node_count)
-    def _():
+    meta_v[...] = jnp.max(far_a[:, 2 * BLOCK :, :].astype(F32), axis=1).astype(jnp.int32)
+    meta_copy.start()
+    for copy in own_copies:
+        copy.wait()
+    meta_copy.wait()
+
+    def node_step(node, carry):
         attend(
-            node_count, nz, step, parents, lengths, spot, meta_s, (far_a, far_b), (acc_a, acc_b),
+            node_count, nz, node, parents, lengths, spot, meta_s, (far_a, far_b), (acc_a, acc_b),
             q_ref, k_ref, v_ref, g_ref, kg_ref, vg_ref, qg_ref,
         )
-
-    @pl.when(step == node_count - 1)
-    def _():
-        send_a[...] = acc_a[...].astype(BF16)
-        send_b[...] = acc_b[...].astype(BF16)
-        for copy in copies_out():
-            copy.start()
-
-    @pl.when(step >= node_count)
-    def _():
-        out_ref[...] = dot(w_ref[...], qg_ref[...], 1, 0).astype(BF16)
-
-    @pl.when(step == pl.num_programs(0) - 1)
-    def _():
-        for copy in copies_out():
-            copy.wait()
+        return carry
+
+    lax.fori_loop(0, node_count, node_step, 0, unroll=UNROLL)
+
+    def convert(i, carry):
+        send_a[i] = acc_a[i].astype(BF16)
+        send_b[i] = acc_b[i].astype(BF16)
+        return carry
+
+    lax.fori_loop(0, NX * nz, convert, 0)
+    for copy in term_copies + grad_copies:
+        copy.start()
+    weight_copy.wait()
+    tile = out_ref.shape[0] // TILES
+
+    def out_copy(i):
+        at = pl.ds(pl.multiple_of(i * tile, tile), tile)
+        return at, pltpu.make_async_copy(out_ref.at[at], out_hbm.at[at], out_sem.at[i])
+
+    def hidden_step(i, carry):
+        at, tile_copy = out_copy(i)
+        out_ref[at, :] = dot(w_ref[at, :], qg_ref[...], 1, 0).astype(BF16)
+        tile_copy.start()
+        return carry
+
+    def hidden_wait(i, carry):
+        out_copy(i)[1].wait()
+        return carry
+
+    lax.fori_loop(0, TILES, hidden_step, 0)
+    for copy in term_copies + grad_copies:
+        copy.wait()
+    lax.fori_loop(0, TILES, hidden_wait, 0)
 
 
 def attend(
@@ -110,6 +136,7 @@
     parent = parents[node]
     link = jnp.where(parent >= 0, lax.div(jnp.maximum(parent, 0), node_count), -1)
     slots, lens = [], [lengths[node]]
+    own_slot = jnp.where(node == 0, 0, NX * nz)
     for _ in range(3):
         slot_a, slot_b = place(link)
         slots.append((slot_a, slot_b))
@@ -127,14 +154,14 @@
         far = far_refs[h]
         acc = acc_refs[h]
         lo, mid, hi = 2 * h * HEAD, (2 * h + 1) * HEAD, (2 * h + 2) * HEAD
-        q = jnp.concatenate([q_ref[:, lo:mid], q_ref[:, mid:hi]], axis=0)
+        q = jnp.concatenate([q_ref[here, lo:mid], q_ref[here, mid:hi]], axis=0)
         zero = jnp.zeros((), BF16)
         g = jnp.concatenate(
-            [jnp.where(live, g_ref[:, lo:mid], zero), jnp.where(live, g_ref[:, mid:hi], zero)], axis=0
+            [jnp.where(live, g_ref[here, lo:mid], zero), jnp.where(live, g_ref[here, mid:hi], zero)], axis=0
         )
         at = slice(h * HEAD, (h + 1) * HEAD)
-        keys = [k_ref[:, at]] + [far[s[h], 0:BLOCK, :] for s in slots]
-        vals = [v_ref[:, at]] + [far[s[h], BLOCK : 2 * BLOCK, :] for s in slots]
+        keys = [k_ref[here, at]] + [far[s[h], 0:BLOCK, :] for s in slots]
+        vals = [v_ref[here, at]] + [far[s[h], BLOCK : 2 * BLOCK, :] for s in slots]
         squash, weight, grad = [], [], []
         total = jnp.zeros((1, cols), F32)
         mixed = jnp.zeros((1, cols), F32)
@@ -157,26 +184,69 @@
             dv = dot(p.astype(BF16), g, 1, 0)
             query_grad += dot(keys[b], ds, 0, 0)
             if b == 0:
-                kg_ref[:, at] = dk.astype(BF16)
-                vg_ref[:, at] = dv.astype(BF16)
-
-                @pl.when(node == 0)
-                def _():
-                    acc[0, 0:BLOCK, :] += dk
-                    acc[0, BLOCK:, :] += dv
-            else:
-                slot = slots[b - 1][h]
-                acc[slot, 0:BLOCK, :] += dk
-                acc[slot, BLOCK:, :] += dv
+                kg_ref[here, at] = dk.astype(BF16)
+                vg_ref[here, at] = dv.astype(BF16)
+
+            slot = slots[b - 1][h] if b else own_slot
+            acc[slot, 0:BLOCK, :] += dk
+            acc[slot, BLOCK:, :] += dv
         qg_ref[lo:mid, here] = query_grad[:, :BLOCK].astype(BF16)
         qg_ref[mid:hi, here] = query_grad[:, BLOCK:].astype(BF16)
 
 
-def local(queries, keys, values, out_grad, query_weight, parents, lengths, *, dp):
+def main_call(nz, parents, lengths, spot, queries, keys, values, out_grad, query_weight, parts):
     node_count = parents.shape[0]
     rows, cols = queries.shape
     kv_cols = keys.shape[1]
     width = query_weight.shape[0]
+    dp = NX * nz
+    half = nz // 2
+    any_spec = pl.BlockSpec(memory_space=pl.ANY)
+    smem = pl.BlockSpec(memory_space=pltpu.SMEM)
+    sizes = [nz, nz, nz, half, half] + [NX] * nz
+    return pl.pallas_call(
+        functools.partial(main_kernel, node_count, nz),
+        in_specs=[smem] * 3 + [any_spec] * (10 + nz),
+        out_specs=[any_spec] * (8 + nz),
+        out_shape=[
+            jax.ShapeDtypeStruct((rows, kv_cols), BF16),
+            jax.ShapeDtypeStruct((rows, kv_cols), BF16),
+            jax.ShapeDtypeStruct((width, rows), BF16),
+        ]
+        + [jax.ShapeDtypeStruct((size, 2 * BLOCK, HEAD), BF16) for size in sizes],
+        scratch_shapes=[
+            pltpu.VMEM((rows, cols), BF16),
+            pltpu.VMEM((rows, kv_cols), BF16),
+            pltpu.VMEM((rows, kv_cols), BF16),
+            pltpu.VMEM((rows, cols), BF16),
+            pltpu.VMEM((width, cols), BF16),
+            pltpu.VMEM((rows, kv_cols), BF16),
+            pltpu.VMEM((rows, kv_cols), BF16),
+            pltpu.VMEM((cols, rows), BF16),
+            pltpu.VMEM((width, rows), BF16),
+            pltpu.VMEM((dp, 2 * BLOCK + META, HEAD), BF16),
+            pltpu.VMEM((dp, 2 * BLOCK, HEAD), BF16),
+            pltpu.VMEM((dp + 1, 2 * BLOCK, HEAD), F32),
+            pltpu.VMEM((dp + 1, 2 * BLOCK, HEAD), F32),
+            pltpu.VMEM((dp, 2 * BLOCK, HEAD), BF16),
+            pltpu.VMEM((dp, 2 * BLOCK, HEAD), BF16),
+            pltpu.VMEM((dp, HEAD), jnp.int32),
+            pltpu.SMEM((dp, HEAD), jnp.int32),
+            pltpu.SemaphoreType.DMA((4,)),
+            pltpu.SemaphoreType.DMA((5 + nz,)),
+            pltpu.SemaphoreType.DMA((5 + nz,)),
+            pltpu.SemaphoreType.DMA((2,)),
+            pltpu.SemaphoreType.DMA((TILES,)),
+            pltpu.SemaphoreType.DMA((2,)),
+        ],
+        compiler_params=pltpu.CompilerParams(vmem_limit_bytes=58 * 1024 * 1024),
+        name="attention",
+    )(parents, lengths, spot, queries, keys, values, out_grad, query_weight, *parts)
+
+
+def local(queries, keys, values, out_grad, query_weight, parents, lengths, *, dp):
+    node_count = parents.shape[0]
+    kv_cols = keys.shape[1]
     nz = dp // NX
     half = nz // 2
 
@@ -221,55 +291,7 @@
     after, before = send(near_a, 1, 0), send(near_a, -1, 0)
     parts = [near_a, after, before, send(after[:half], 1, 0), send(before[half:], -1, 0)] + rings
 
-    any_spec = pl.BlockSpec(memory_space=pl.ANY)
-    tiles = 8
-    tile = width // tiles
-    node_map = lambda i: (jnp.minimum(i, node_count - 1), 0)
-    tile_map = lambda i: (jnp.maximum(i - node_count, 0), 0)
-    sizes = [nz, nz, nz, half, half] + [NX] * nz
-    outs = pl.pallas_call(
-        functools.partial(main_kernel, node_count, nz),
-        grid=(node_count + tiles,),
-        in_specs=[
-            smem,
-            smem,
-            smem,
-            pl.BlockSpec((BLOCK, cols), node_map),
-            pl.BlockSpec((BLOCK, kv_cols), node_map),
-            pl.BlockSpec((BLOCK, kv_cols), node_map),
-            pl.BlockSpec((BLOCK, cols), node_map),
-            pl.BlockSpec((tile, cols), tile_map),
-        ]
-        + [any_spec] * (5 + nz),
-        out_specs=[
-            pl.BlockSpec((BLOCK, kv_cols), node_map),
-            pl.BlockSpec((BLOCK, kv_cols), node_map),
-            pl.BlockSpec((tile, rows), tile_map),
-        ]
-        + [any_spec] * (5 + nz),
-        out_shape=[
-            jax.ShapeDtypeStruct((rows, kv_cols), BF16),
-            jax.ShapeDtypeStruct((rows, kv_cols), BF16),
-            jax.ShapeDtypeStruct((width, rows), BF16),
-        ]
-        + [jax.ShapeDtypeStruct((size, 2 * BLOCK, HEAD), BF16) for size in sizes],
-        scratch_shapes=[
-            pltpu.VMEM((dp, 2 * BLOCK + META, HEAD), BF16),
-            pltpu.VMEM((dp, 2 * BLOCK, HEAD), BF16),
-            pltpu.VMEM((dp, 2 * BLOCK, HEAD), F32),
-            pltpu.VMEM((dp, 2 * BLOCK, HEAD), F32),
-            pltpu.VMEM((dp, 2 * BLOCK, HEAD), BF16),
-            pltpu.VMEM((dp, 2 * BLOCK, HEAD), BF16),
-            pltpu.VMEM((cols, rows), BF16),
-            pltpu.VMEM((dp, HEAD), jnp.int32),
-            pltpu.SMEM((dp, HEAD), jnp.int32),
-            pltpu.SemaphoreType.DMA((5 + nz,)),
-            pltpu.SemaphoreType.DMA((5 + nz,)),
-            pltpu.SemaphoreType.DMA,
-        ],
-        compiler_params=pltpu.CompilerParams(vmem_limit_bytes=58 * 1024 * 1024),
-        name="attention",
-    )(parents, lengths, spot, queries, keys, values, out_grad, query_weight, *parts)
+    outs = main_call(nz, parents, lengths, spot, queries, keys, values, out_grad, query_weight, parts)
     key_grad, value_grad, hidden = outs[:3]
     own, prev, succ, far_low, far_high = outs[3:8]
     terms = outs[8:]

time: 157 us -> 152 us (0.968)
  Pallas kernels: 26.4 us -> 21.3 us
    pallas_call x1, Pallas kernels: 24.8 us -> 19.7 us  [main_call(): pl.pallas_call(functools.partial(main_kernel, node_count, nz), in_specs=[...]
where the time goes in v1:
time: 152 us
  starting transfers between devices  58.7 us (39%)
  waiting for transfers between devices  52.9 us (35%)
  Pallas kernels  21.3 us (14%)
  between operations  14.5 us (10%)
  other arithmetic  3.22 us (2%)
    ppermute x40, starting transfers between devices, send(): return lax.ppermute(array, 'dp', pairs)  58.6 us
    ppermute x40, waiting for transfers between devices, send(): return lax.ppermute(array, 'dp', pairs)  52.9 us
    pallas_call x1, Pallas kernels, main_call(): pl.pallas_call(functools.partial(main_kernel, node_count, nz), in_specs=[...  19.7 us
  transfers between devices with their start and end apart: 41, of which 19 were waited for; matrix products, arithmetic and copies ran while one was open for 3% of the time, Pallas kernels for 0%

profile of v1, /device:TPU:16, one launch (start us, length us, event | category | flops | bytes accessed | tf_op | source)
XLA Modules:
  0.0 151.7 jit_solution(7363316882065351954)
XLA Ops:
  7.2 1.6 %pack.1 = (bf16[272,128]{1,0:T(8,128)(2,1)}, bf16[256,128]{1,0:T(8,128)(2,1)}) custom-call(s32[6]{0:T(128)} %parents.3, s32[6]{0:T(128)} %lengths.3, bf16[768,256]{1,0:T(8,128)(2,1)} %k_hbm.1, bf16[768,256]{1,0:T(8,128)(2,1)} %v_hbm.1), custom_call_target="tpu_custom_call" | custom-call | tf_op jit(solution)/shard_map/pack/pallas_call | solution.py:265
  8.8 2.8 %collective-permute-start.12 = (bf16[256,128]{1,0:T(8,128)(2,1)}, bf16[256,128]{1,0:T(8,128)(2,1)S(1)}, u32[]{:S(2)}, u32[]{:S(2)}) collective-permute-start(bf16[256,128]{1,0:T(8,128)(2,1)} %get-tuple-element.22), channel_id=1, source_target_pairs={{0,192},{8,200},{16,208},{24,216},{32,224},{40,232},{48,240},{56,2... | collective-permute-start | bytes 196616 | tf_op jit(solution)/shard_map/ppermute | solution.py:257
  11.5 0.8 collective-permute-start.11
  12.3 0.9 collective-permute-start.10
  13.2 6.3 %collective-permute-start.5 = (bf16[272,128]{1,0:T(8,128)(2,1)}, bf16[272,128]{1,0:T(8,128)(2,1)S(1)}, u32[]{:S(2)}, u32[]{:S(2)}) collective-permute-start(bf16[272,128]{1,0:T(8,128)(2,1)} %get-tuple-element.21), channel_id=1, source_target_pairs={{0,48},{8,56},{16,0},{24,8},{32,16},{40,24},{48,32},{56,40},{64,11... | collective-permute-start | bytes 208904 | tf_op jit(solution)/shard_map/ppermute | solution.py:257
  19.5 1.0 collective-permute-start.3
  20.5 0.9 bitcast_dynamic-update-slice_fusion.3
  21.5 1.5 %collective-permute-start.1 = (bf16[272,128]{1,0:T(8,128)(2,1)}, bf16[272,128]{1,0:T(8,128)(2,1)S(1)}, u32[]{:S(2)}, u32[]{:S(2)}) collective-permute-start(bf16[272,128]{1,0:T(8,128)(2,1)} %get-tuple-element.21), channel_id=1, source_target_pairs={{0,16},{8,24},{16,32},{24,40},{32,48},{40,56},{48,0},{56,8},{64,80... | collective-permute-start | bytes 208904 | tf_op jit(solution)/shard_map/ppermute | solution.py:257
  23.0 0.9 pad_maximum_fusion.2.refs_5_
  23.9 0.7 collective-permute-start.13
  24.6 4.9 %collective-permute-done.1 = bf16[272,128]{1,0:T(8,128)(2,1)S(1)} collective-permute-done((bf16[272,128]{1,0:T(8,128)(2,1)}, bf16[272,128]{1,0:T(8,128)(2,1)S(1)}, u32[]{:S(2)}, u32[]{:S(2)}) %collective-permute-start.1) | collective-permute-done | bytes 69664 | tf_op jit(solution)/shard_map/ppermute | solution.py:257
  29.6 1.2 collective-permute-done
  30.8 0.1 collective-permute-start.2
  30.9 4.1 %collective-permute-start.4 = (bf16[272,128]{1,0:T(8,128)(2,1)S(1)}, bf16[272,128]{1,0:T(8,128)(2,1)S(1)}, u32[]{:S(2)}, u32[]{:S(2)}) collective-permute-start(bf16[272,128]{1,0:T(8,128)(2,1)S(1)} %collective-permute-done.3), channel_id=1, source_target_pairs={{0,48},{8,56},{16,0},{24,8},{32,16},{40,24},{48,32},{56,40},{64,11... | collective-permute-start | bytes 208904 | tf_op jit(solution)/shard_map/ppermute | solution.py:257
  35.0 5.9 %collective-permute-done.2 = bf16[2,272,128]{2,1,0:T(8,128)(2,1)S(1)} collective-permute-done((bf16[2,272,128]{2,1,0:T(8,128)(2,1)S(1)}, bf16[2,272,128]{2,1,0:T(8,128)(2,1)S(1)}, u32[]{:S(2)}, u32[]{:S(2)}) %collective-permute-start.2) | collective-permute-done | bytes 139296 | tf_op jit(solution)/shard_map/ppermute | solution.py:257
  41.0 2.4 %collective-permute-start.7 = (bf16[8,272,128]{2,1,0:T(8,128)(2,1)S(1)}, bf16[8,272,128]{2,1,0:T(8,128)(2,1)S(1)}, u32[]{:S(2)}, u32[]{:S(2)}) collective-permute-start(bf16[8,272,128]{2,1,0:T(8,128)(2,1)S(1)} %bitcast_dynamic-update-slice_fusion.refs_0_), channel_id=1, source_target_pairs={{0,192},{8,200},{16,208},{24,216},{32,224},{40,232},{48,240},{56,2... | collective-permute-start | bytes 1671176 | tf_op jit(solution)/shard_map/ppermute | solution.py:257
  43.5 2.0 %collective-permute-start.14 = (bf16[4,256,128]{2,1,0:T(8,128)(2,1)S(1)}, bf16[4,256,128]{2,1,0:T(8,128)(2,1)S(1)}, u32[]{:S(2)}, u32[]{:S(2)}) collective-permute-start(bf16[4,256,128]{2,1,0:T(8,128)(2,1)S(1)} %collective-permute-done.13.refs_6_), channel_id=1, source_target_pairs={{0,8},{8,16},{16,24},{24,32},{32,40},{40,48},{48,56},{56,0},{64,72... | collective-permute-start | bytes 786440 | tf_op jit(solution)/shard_map/ppermute | solution.py:257
  45.5 6.3 %collective-permute-done.17.refs_12_ = bf16[4,256,128]{2,1,0:T(8,128)(2,1)S(1)} collective-permute-done((bf16[4,256,128]{2,1,0:T(8,128)(2,1)S(1)}, bf16[4,256,128]{2,1,0:T(8,128)(2,1)S(1)}, u32[]{:S(2)}, u32[]{:S(2)}) %collective-permute-start.17) | collective-permute-done | bytes 262176 | tf_op jit(solution)/shard_map/ppermute | solution.py:257
  51.8 0.3 collective-permute-done.14.refs_7_
  52.1 2.1 %collective-permute-start.15 = (bf16[4,256,128]{2,1,0:T(8,128)(2,1)S(1)}, bf16[4,256,128]{2,1,0:T(8,128)(2,1)}, u32[]{:S(2)}, u32[]{:S(2)}) collective-permute-start(bf16[4,256,128]{2,1,0:T(8,128)(2,1)S(1)} %collective-permute-done.14.refs_7_), channel_id=1, source_target_pairs={{0,8},{8,16},{16,24},{24,32},{32,40},{40,48},{48,56},{56,0},{64,72... | collective-permute-start | bytes 786440 | tf_op jit(solution)/shard_map/ppermute | solution.py:257
  54.2 3.5 %collective-permute-start.9 = (bf16[4,272,128]{2,1,0:T(8,128)(2,1)S(1)}, bf16[4,272,128]{2,1,0:T(8,128)(2,1)S(1)}, u32[]{:S(2)}, u32[]{:S(2)}) collective-permute-start(bf16[4,272,128]{2,1,0:T(8,128)(2,1)S(1)} %slice.193), channel_id=1, source_target_pairs={{0,192},{8,200},{16,208},{24,216},{32,224},{40,232},{48,240},{56,2... | collective-permute-start | bytes 835592 | tf_op jit(solution)/shard_map/ppermute | solution.py:257
  57.7 0.1 collective-permute-start.8
  57.8 3.1 %collective-permute-done.18.refs_11_ = bf16[4,256,128]{2,1,0:T(8,128)(2,1)} collective-permute-done((bf16[4,256,128]{2,1,0:T(8,128)(2,1)S(1)}, bf16[4,256,128]{2,1,0:T(8,128)(2,1)}, u32[]{:S(2)}, u32[]{:S(2)}) %collective-permute-start.18) | collective-permute-done | bytes 262176 | tf_op jit(solution)/shard_map/ppermute | solution.py:257
  60.9 0.4 collective-permute-done.15.refs_8_
  61.4 1.9 %collective-permute-start.16 = (bf16[4,256,128]{2,1,0:T(8,128)(2,1)}, bf16[4,256,128]{2,1,0:T(8,128)(2,1)}, u32[]{:S(2)}, u32[]{:S(2)}) collective-permute-start(bf16[4,256,128]{2,1,0:T(8,128)(2,1)} %collective-permute-done.15.refs_8_), channel_id=1, source_target_pairs={{0,8},{8,16},{16,24},{24,32},{32,40},{40,48},{48,56},{56,0},{64,72... | collective-permute-start | bytes 786440 | tf_op jit(solution)/shard_map/ppermute | solution.py:257
  63.3 0.6 pad_add_fusion.spot
  63.9 3.7 %collective-permute-done.19.refs_10_ = bf16[4,256,128]{2,1,0:T(8,128)(2,1)} collective-permute-done((bf16[4,256,128]{2,1,0:T(8,128)(2,1)}, bf16[4,256,128]{2,1,0:T(8,128)(2,1)}, u32[]{:S(2)}, u32[]{:S(2)}) %collective-permute-start.19) | collective-permute-done | bytes 262176 | tf_op jit(solution)/shard_map/ppermute | solution.py:257
  67.6 1.6 %collective-permute-done.16.refs_9_ = bf16[4,256,128]{2,1,0:T(8,128)(2,1)} collective-permute-done((bf16[4,256,128]{2,1,0:T(8,128)(2,1)}, bf16[4,256,128]{2,1,0:T(8,128)(2,1)}, u32[]{:S(2)}, u32[]{:S(2)}) %collective-permute-start.16) | collective-permute-done | bytes 262176 | tf_op jit(solution)/shard_map/ppermute | solution.py:257
  69.3 19.7 %attention.1 = (bf16[768,256]{1,0:T(8,128)(2,1)}, bf16[768,256]{1,0:T(8,128)(2,1)}, bf16[4608,768]{1,0:T(8,128)(2,1)}, bf16[8,256,128]{2,1,0:T(8,128)(2,1)}, bf1...) custom-call(s32[6]{0:T(128)} %parents.3, ...), custom_call_target="tpu_custom_call" | custom-call | tf_op jit(solution)/shard_map/attention/pallas_call | solution.py:207
  89.1 2.9 %collective-permute-start.22 = (bf16[4,256,128]{2,1,0:T(8,128)(2,1)}, bf16[4,256,128]{2,1,0:T(8,128)(2,1)S(1)}, u32[]{:S(2)}, u32[]{:S(2)}) collective-permute-start(bf16[4,256,128]{2,1,0:T(8,128)(2,1)} %get-tuple-element.28), channel_id=1, source_target_pairs={{0,64},{8,72},{16,80},{24,88},{32,96},{40,104},{48,112},{56,120},{... | collective-permute-start | bytes 786440 | tf_op jit(solution)/shard_map/ppermute | solution.py:257
  92.2 2.3 %collective-permute-start.20 = (bf16[4,256,128]{2,1,0:T(8,128)(2,1)}, bf16[4,256,128]{2,1,0:T(8,128)(2,1)S(1)}, u32[]{:S(2)}, u32[]{:S(2)}) collective-permute-start(bf16[4,256,128]{2,1,0:T(8,128)(2,1)} %get-tuple-element.26), channel_id=1, source_target_pairs={{0,192},{8,200},{16,208},{24,216},{32,224},{40,232},{48,240},{56,2... | collective-permute-start | bytes 786440 | tf_op jit(solution)/shard_map/ppermute | solution.py:257
  94.5 0.2 collective-permute-start.30
  94.7 1.8 %collective-permute-start.34 = (bf16[4,256,128]{2,1,0:T(8,128)(2,1)S(1)}, bf16[4,256,128]{2,1,0:T(8,128)(2,1)S(1)}, u32[]{:S(2)}, u32[]{:S(2)}) collective-permute-start(bf16[4,256,128]{2,1,0:T(8,128)(2,1)S(1)} %copy-done.18), channel_id=1, source_target_pairs={{0,8},{8,16},{16,24},{24,32},{32,40},{40,48},{48,56},{56,0},{64,72... | collective-permute-start | bytes 786440 | tf_op jit(solution)/shard_map/ppermute | solution.py:257
  96.5 4.3 %collective-permute-done.22 = bf16[4,256,128]{2,1,0:T(8,128)(2,1)S(1)} collective-permute-done((bf16[4,256,128]{2,1,0:T(8,128)(2,1)}, bf16[4,256,128]{2,1,0:T(8,128)(2,1)S(1)}, u32[]{:S(2)}, u32[]{:S(2)}) %collective-permute-start.22) | collective-permute-done | bytes 262176 | tf_op jit(solution)/shard_map/ppermute | solution.py:257
  100.9 0.4 collective-permute-start.23
  101.3 0.3 collective-permute-done.20
  101.7 3.6 %collective-permute-start.21 = (bf16[8,256,128]{2,1,0:T(8,128)(2,1)S(1)}, bf16[8,256,128]{2,1,0:T(8,128)(2,1)S(1)}, u32[]{:S(2)}, u32[]{:S(2)}) collective-permute-start(bf16[8,256,128]{2,1,0:T(8,128)(2,1)S(1)} %pad_maximum_fusion), channel_id=1, source_target_pairs={{0,192},{8,200},{16,208},{24,216},{32,224},{40,232},{48,240},{56,2... | collective-permute-start | bytes 1572872 | tf_op jit(solution)/shard_map/ppermute | solution.py:257
  105.4 0.3 collective-permute-start.31
  105.8 2.1 %collective-permute-start.35 = (bf16[4,256,128]{2,1,0:T(8,128)(2,1)S(1)}, bf16[4,256,128]{2,1,0:T(8,128)(2,1)S(1)}, u32[]{:S(2)}, u32[]{:S(2)}) collective-permute-start(bf16[4,256,128]{2,1,0:T(8,128)(2,1)S(1)} %add_convert_fusion.1), channel_id=1, source_target_pairs={{0,8},{8,16},{16,24},{24,32},{32,40},{40,48},{48,56},{56,0},{64,72... | collective-permute-start | bytes 786440 | tf_op jit(solution)/shard_map/ppermute | solution.py:257
  107.9 4.2 %collective-permute-done.31 = bf16[4,256,128]{2,1,0:T(8,128)(2,1)S(1)} collective-permute-done((bf16[4,256,128]{2,1,0:T(8,128)(2,1)S(1)}, bf16[4,256,128]{2,1,0:T(8,128)(2,1)S(1)}, u32[]{:S(2)}, u32[]{:S(2)}) %collective-permute-start.31) | collective-permute-done | bytes 262176 | tf_op jit(solution)/shard_map/ppermute | solution.py:257
  112.2 3.0 %collective-permute-start.32 = (bf16[4,256,128]{2,1,0:T(8,128)(2,1)S(1)}, bf16[4,256,128]{2,1,0:T(8,128)(2,1)S(1)}, u32[]{:S(2)}, u32[]{:S(2)}) collective-permute-start(bf16[4,256,128]{2,1,0:T(8,128)(2,1)S(1)} %add_convert_fusion.3), channel_id=1, source_target_pairs={{0,56},{8,0},{16,8},{24,16},{32,24},{40,32},{48,40},{56,48},{64,12... | collective-permute-start | bytes 786440 | tf_op jit(solution)/shard_map/ppermute | solution.py:257
  115.3 0.1 collective-permute-start.24
  115.4 0.1 add_convert_fusion
  115.4 1.5 %collective-permute-start.36 = (bf16[4,256,128]{2,1,0:T(8,128)(2,1)S(1)}, bf16[4,256,128]{2,1,0:T(8,128)(2,1)S(1)}, u32[]{:S(2)}, u32[]{:S(2)}) collective-permute-start(bf16[4,256,128]{2,1,0:T(8,128)(2,1)S(1)} %add_convert_fusion), channel_id=1, source_target_pairs={{0,8},{8,16},{16,24},{24,32},{32,40},{40,48},{48,56},{56,0},{64,72... | collective-permute-start | bytes 786440 | tf_op jit(solution)/shard_map/ppermute | solution.py:257
  117.0 9.0 %collective-permute-done.24 = bf16[2,256,128]{2,1,0:T(8,128)(2,1)S(1)} collective-permute-done((bf16[2,256,128]{2,1,0:T(8,128)(2,1)S(1)}, bf16[2,256,128]{2,1,0:T(8,128)(2,1)S(1)}, u32[]{:S(2)}, u32[]{:S(2)}) %collective-permute-start.24) | collective-permute-done | bytes 131104 | tf_op jit(solution)/shard_map/ppermute | solution.py:257
  126.0 0.1 fusion.16
  126.1 3.0 %collective-permute-start.28 = (bf16[256,128]{1,0:T(8,128)(2,1)S(1)}, bf16[256,128]{1,0:T(8,128)(2,1)S(1)}, u32[]{:S(2)}, u32[]{:S(2)}) collective-permute-start(bf16[256,128]{1,0:T(8,128)(2,1)S(1)} %get-tuple-element.41), channel_id=1, source_target_pairs={{0,16},{8,24},{16,32},{24,40},{32,48},{40,56},{48,0},{56,8},{64,80... | collective-permute-start | bytes 196616 | tf_op jit(solution)/shard_map/ppermute | solution.py:257
  129.1 0.1 add_convert_fusion.2
  129.2 0.1 collective-permute-start.33
  129.3 1.7 %collective-permute-start.25 = (bf16[256,128]{1,0:T(8,128)(2,1)S(1)}, bf16[256,128]{1,0:T(8,128)(2,1)S(1)}, u32[]{:S(2)}, u32[]{:S(2)}) collective-permute-start(bf16[256,128]{1,0:T(8,128)(2,1)S(1)} %get-tuple-element.39), channel_id=1, source_target_pairs={{0,56},{8,0},{16,8},{24,16},{32,24},{40,32},{48,40},{56,48},{64,12... | collective-permute-start | bytes 196616 | tf_op jit(solution)/shard_map/ppermute | solution.py:257
  131.0 2.9 %collective-permute-start.26 = (bf16[256,128]{1,0:T(8,128)(2,1)S(1)}, bf16[256,128]{1,0:T(8,128)(2,1)S(1)}, u32[]{:S(2)}, u32[]{:S(2)}) collective-permute-start(bf16[256,128]{1,0:T(8,128)(2,1)S(1)} %get-tuple-element.40), channel_id=1, source_target_pairs={{0,48},{8,56},{16,0},{24,8},{32,16},{40,24},{48,32},{56,40},{64,11... | collective-permute-start | bytes 196616 | tf_op jit(solution)/shard_map/ppermute | solution.py:257
  133.9 0.4 collective-permute-start.27
  134.4 0.1 collective-permute-start.29
  134.5 1.6 %collective-permute-done.33 = bf16[4,256,128]{2,1,0:T(8,128)(2,1)S(1)} collective-permute-done((bf16[4,256,128]{2,1,0:T(8,128)(2,1)S(1)}, bf16[4,256,128]{2,1,0:T(8,128)(2,1)S(1)}, u32[]{:S(2)}, u32[]{:S(2)}) %collective-permute-start.33) | collective-permute-done | bytes 262176 | tf_op jit(solution)/shard_map/ppermute | solution.py:257
  136.1 0.1 fusion.13
  136.2 0.3 collective-permute-start.37
  136.6 0.5 collective-permute-done.25
  137.1 1.2 collective-permute-start.39
  138.3 0.2 collective-permute-start.38
  138.6 1.8 %collective-permute-done.27 = bf16[256,128]{1,0:T(8,128)(2,1)S(1)} collective-permute-done((bf16[256,128]{1,0:T(8,128)(2,1)S(1)}, bf16[256,128]{1,0:T(8,128)(2,1)S(1)}, u32[]{:S(2)}, u32[]{:S(2)}) %collective-permute-start.27) | collective-permute-done | bytes 65568 | tf_op jit(solution)/shard_map/ppermute | solution.py:257
  140.4 0.2 collective-permute-done.29
  140.7 1.8 %collective-permute-done.39 = bf16[256,128]{1,0:T(8,128)(2,1)S(1)} collective-permute-done((bf16[256,128]{1,0:T(8,128)(2,1)S(1)}, bf16[256,128]{1,0:T(8,128)(2,1)S(1)}, u32[]{:S(2)}, u32[]{:S(2)}) %collective-permute-start.39) | collective-permute-done | bytes 65568 | tf_op jit(solution)/shard_map/ppermute | solution.py:257
  142.6 1.5 %collective-permute-done.38 = bf16[256,128]{1,0:T(8,128)(2,1)S(1)} collective-permute-done((bf16[256,128]{1,0:T(8,128)(2,1)S(1)}, bf16[256,128]{1,0:T(8,128)(2,1)S(1)}, u32[]{:S(2)}, u32[]{:S(2)}) %collective-permute-start.38) | collective-permute-done | bytes 65568 | tf_op jit(solution)/shard_map/ppermute | solution.py:257
  144.2 0.7 maximum_dynamic-update-slice_fusion
  (94 shorter events, 1.1 us)
Async XLA Ops:
  7.2 137.7 %reduce-scatter.2.cloned.1.call-start = ((), (), s32[]{:S(2)}) async-start(), calls=%async_computation.1 | async-start | bytes 7962624 | tf_op jit(solution)/shard_map/reduce_scatter | solution.py:299
  8.8 12.7 %collective-permute-start.12 = (bf16[256,128]{1,0:T(8,128)(2,1)}, bf16[256,128]{1,0:T(8,128)(2,1)S(1)}, u32[]{:S(2)}, u32[]{:S(2)}) collective-permute-start(bf16[256,128]{1,0:T(8,128)(2,1)} %get-tuple-element.22), channel_id=1, source_target_pairs={{0,192},{8,200},{16,208},{24,216},{32,224},{40,232},{48,240},{56,2... | collective-permute-start | bytes 196616 | tf_op jit(solution)/shard_map/ppermute | solution.py:257
  11.5 11.5 %collective-permute-start.11 = (bf16[256,128]{1,0:T(8,128)(2,1)}, bf16[256,128]{1,0:T(8,128)(2,1)S(1)}, u32[]{:S(2)}, u32[]{:S(2)}) collective-permute-start(bf16[256,128]{1,0:T(8,128)(2,1)} %get-tuple-element.22), channel_id=1, source_target_pairs={{0,128},{8,136},{16,144},{24,152},{32,160},{40,168},{48,176},{56,1... | collective-permute-start | bytes 196616 | tf_op jit(solution)/shard_map/ppermute | solution.py:257
  12.3 10.7 %collective-permute-start.10 = (bf16[256,128]{1,0:T(8,128)(2,1)}, bf16[256,128]{1,0:T(8,128)(2,1)S(1)}, u32[]{:S(2)}, u32[]{:S(2)}) collective-permute-start(bf16[256,128]{1,0:T(8,128)(2,1)} %get-tuple-element.22), channel_id=1, source_target_pairs={{0,64},{8,72},{16,80},{24,88},{32,96},{40,104},{48,112},{56,120},{... | collective-permute-start | bytes 196616 | tf_op jit(solution)/shard_map/ppermute | solution.py:257
  13.2 27.7 %collective-permute-start.5 = (bf16[272,128]{1,0:T(8,128)(2,1)}, bf16[272,128]{1,0:T(8,128)(2,1)S(1)}, u32[]{:S(2)}, u32[]{:S(2)}) collective-permute-start(bf16[272,128]{1,0:T(8,128)(2,1)} %get-tuple-element.21), channel_id=1, source_target_pairs={{0,48},{8,56},{16,0},{24,8},{32,16},{40,24},{48,32},{56,40},{64,11... | collective-permute-start | bytes 208904 | tf_op jit(solution)/shard_map/ppermute | solution.py:257
  19.5 11.4 %collective-permute-start.3 = (bf16[272,128]{1,0:T(8,128)(2,1)}, bf16[272,128]{1,0:T(8,128)(2,1)S(1)}, u32[]{:S(2)}, u32[]{:S(2)}) collective-permute-start(bf16[272,128]{1,0:T(8,128)(2,1)} %get-tuple-element.21), channel_id=1, source_target_pairs={{0,56},{8,0},{16,8},{24,16},{32,24},{40,32},{48,40},{56,48},{64,12... | collective-permute-start | bytes 208904 | tf_op jit(solution)/shard_map/ppermute | solution.py:257
  21.5 8.1 %collective-permute-start.1 = (bf16[272,128]{1,0:T(8,128)(2,1)}, bf16[272,128]{1,0:T(8,128)(2,1)S(1)}, u32[]{:S(2)}, u32[]{:S(2)}) collective-permute-start(bf16[272,128]{1,0:T(8,128)(2,1)} %get-tuple-element.21), channel_id=1, source_target_pairs={{0,16},{8,24},{16,32},{24,40},{32,48},{40,56},{48,0},{56,8},{64,80... | collective-permute-start | bytes 208904 | tf_op jit(solution)/shard_map/ppermute | solution.py:257
  23.0 7.8 %collective-permute-start = (bf16[272,128]{1,0:T(8,128)(2,1)}, bf16[272,128]{1,0:T(8,128)(2,1)S(1)}, u32[]{:S(2)}, u32[]{:S(2)}) collective-permute-start(bf16[272,128]{1,0:T(8,128)(2,1)} %get-tuple-element.21), channel_id=1, source_target_pairs={{0,8},{8,16},{16,24},{24,32},{32,40},{40,48},{48,56},{56,0},{64,72... | collective-permute-start | bytes 208904 | tf_op jit(solution)/shard_map/ppermute | solution.py:257
  23.9 45.4 %copy-start.2 = (bf16[4,256,128]{2,1,0:T(8,128)(2,1)}, bf16[4,256,128]{2,1,0:T(8,128)(2,1)S(1)}, u32[]{:S(2)}) copy-start(bf16[4,256,128]{2,1,0:T(8,128)(2,1)S(1)} %pad_maximum_fusion.2.refs_5_) | copy-start | bytes 786436
  23.9 19.5 %collective-permute-start.13 = (bf16[4,256,128]{2,1,0:T(8,128)(2,1)S(1)}, bf16[4,256,128]{2,1,0:T(8,128)(2,1)S(1)}, u32[]{:S(2)}, u32[]{:S(2)}) collective-permute-start(bf16[4,256,128]{2,1,0:T(8,128)(2,1)S(1)} %pad_maximum_fusion.2.refs_5_), channel_id=1, source_target_pairs={{0,8},{8,16},{16,24},{24,32},{32,40},{40,48},{48,56},{56,0},{64,72... | collective-permute-start | bytes 786440 | tf_op jit(solution)/shard_map/ppermute | solution.py:257
  30.8 10.1 %collective-permute-start.2 = (bf16[2,272,128]{2,1,0:T(8,128)(2,1)S(1)}, bf16[2,272,128]{2,1,0:T(8,128)(2,1)S(1)}, u32[]{:S(2)}, u32[]{:S(2)}) collective-permute-start(bf16[2,272,128]{2,1,0:T(8,128)(2,1)S(1)} %pad_maximum_fusion.3), channel_id=1, source_target_pairs={{0,16},{8,24},{16,32},{24,40},{32,48},{40,56},{48,0},{56,8},{64,80... | collective-permute-start | bytes 417800 | tf_op jit(solution)/shard_map/ppermute | solution.py:257
  30.9 10.0 %collective-permute-start.4 = (bf16[272,128]{1,0:T(8,128)(2,1)S(1)}, bf16[272,128]{1,0:T(8,128)(2,1)S(1)}, u32[]{:S(2)}, u32[]{:S(2)}) collective-permute-start(bf16[272,128]{1,0:T(8,128)(2,1)S(1)} %collective-permute-done.3), channel_id=1, source_target_pairs={{0,48},{8,56},{16,0},{24,8},{32,16},{40,24},{48,32},{56,40},{64,11... | collective-permute-start | bytes 208904 | tf_op jit(solution)/shard_map/ppermute | solution.py:257
  41.0 28.3 %copy-start.3 = (bf16[8,272,128]{2,1,0:T(8,128)(2,1)}, bf16[8,272,128]{2,1,0:T(8,128)(2,1)S(1)}, u32[]{:S(2)}) copy-start(bf16[8,272,128]{2,1,0:T(8,128)(2,1)S(1)} %bitcast_dynamic-update-slice_fusion.refs_0_) | copy-start | bytes 1671172
  41.0 13.2 %collective-permute-start.7 = (bf16[8,272,128]{2,1,0:T(8,128)(2,1)S(1)}, bf16[8,272,128]{2,1,0:T(8,128)(2,1)S(1)}, u32[]{:S(2)}, u32[]{:S(2)}) collective-permute-start(bf16[8,272,128]{2,1,0:T(8,128)(2,1)S(1)} %bitcast_dynamic-update-slice_fusion.refs_0_), channel_id=1, source_target_pairs={{0,192},{8,200},{16,208},{24,216},{32,224},{40,232},{48,240},{56,2... | collective-permute-start | bytes 1671176 | tf_op jit(solution)/shard_map/ppermute | solution.py:257
  43.4 14.3 %collective-permute-start.6 = (bf16[8,272,128]{2,1,0:T(8,128)(2,1)S(1)}, bf16[8,272,128]{2,1,0:T(8,128)(2,1)S(1)}, u32[]{:S(2)}, u32[]{:S(2)}) collective-permute-start(bf16[8,272,128]{2,1,0:T(8,128)(2,1)S(1)} %bitcast_dynamic-update-slice_fusion.refs_0_), channel_id=1, source_target_pairs={{0,64},{8,72},{16,80},{24,88},{32,96},{40,104},{48,112},{56,120},{... | collective-permute-start | bytes 1671176 | tf_op jit(solution)/shard_map/ppermute | solution.py:257
  43.4 8.4 %collective-permute-start.17 = (bf16[4,256,128]{2,1,0:T(8,128)(2,1)S(1)}, bf16[4,256,128]{2,1,0:T(8,128)(2,1)S(1)}, u32[]{:S(2)}, u32[]{:S(2)}) collective-permute-start(bf16[4,256,128]{2,1,0:T(8,128)(2,1)S(1)} %pad_maximum_fusion.2.refs_5_), channel_id=1, source_target_pairs={{0,56},{8,0},{16,8},{24,16},{32,24},{40,32},{48,40},{56,48},{64,12... | collective-permute-start | bytes 786440 | tf_op jit(solution)/shard_map/ppermute | solution.py:257
  43.4 25.8 %copy-start.9 = (bf16[4,256,128]{2,1,0:T(8,128)(2,1)}, bf16[4,256,128]{2,1,0:T(8,128)(2,1)S(1)}, u32[]{:S(2)}) copy-start(bf16[4,256,128]{2,1,0:T(8,128)(2,1)S(1)} %collective-permute-done.13.refs_6_) | copy-start | bytes 786436
  43.5 8.6 %collective-permute-start.14 = (bf16[4,256,128]{2,1,0:T(8,128)(2,1)S(1)}, bf16[4,256,128]{2,1,0:T(8,128)(2,1)S(1)}, u32[]{:S(2)}, u32[]{:S(2)}) collective-permute-start(bf16[4,256,128]{2,1,0:T(8,128)(2,1)S(1)} %collective-permute-done.13.refs_6_), channel_id=1, source_target_pairs={{0,8},{8,16},{16,24},{24,32},{32,40},{40,48},{48,56},{56,0},{64,72... | collective-permute-start | bytes 786440 | tf_op jit(solution)/shard_map/ppermute | solution.py:257
  51.8 6.0 %copy-start.11 = (bf16[4,256,128]{2,1,0:T(8,128)(2,1)}, bf16[4,256,128]{2,1,0:T(8,128)(2,1)S(1)}, u32[]{:S(2)}) copy-start(bf16[4,256,128]{2,1,0:T(8,128)(2,1)S(1)} %collective-permute-done.17.refs_12_) | copy-start | bytes 786436
  51.8 9.1 %collective-permute-start.18 = (bf16[4,256,128]{2,1,0:T(8,128)(2,1)S(1)}, bf16[4,256,128]{2,1,0:T(8,128)(2,1)}, u32[]{:S(2)}, u32[]{:S(2)}) collective-permute-start(bf16[4,256,128]{2,1,0:T(8,128)(2,1)S(1)} %collective-permute-done.17.refs_12_), channel_id=1, source_target_pairs={{0,56},{8,0},{16,8},{24,16},{32,24},{40,32},{48,40},{56,48},{64,12... | collective-permute-start | bytes 786440 | tf_op jit(solution)/shard_map/ppermute | solution.py:257
  52.1 8.8 %copy-start.12 = (bf16[4,256,128]{2,1,0:T(8,128)(2,1)}, bf16[4,256,128]{2,1,0:T(8,128)(2,1)S(1)}, u32[]{:S(2)}) copy-start(bf16[4,256,128]{2,1,0:T(8,128)(2,1)S(1)} %collective-permute-done.14.refs_7_) | copy-start | bytes 786436
  52.1 9.3 %collective-permute-start.15 = (bf16[4,256,128]{2,1,0:T(8,128)(2,1)S(1)}, bf16[4,256,128]{2,1,0:T(8,128)(2,1)}, u32[]{:S(2)}, u32[]{:S(2)}) collective-permute-start(bf16[4,256,128]{2,1,0:T(8,128)(2,1)S(1)} %collective-permute-done.14.refs_7_), channel_id=1, source_target_pairs={{0,8},{8,16},{16,24},{24,32},{32,40},{40,48},{48,56},{56,0},{64,72... | collective-permute-start | bytes 786440 | tf_op jit(solution)/shard_map/ppermute | solution.py:257
  54.2 15.1 %copy-start = (bf16[8,272,128]{2,1,0:T(8,128)(2,1)}, bf16[8,272,128]{2,1,0:T(8,128)(2,1)S(1)}, u32[]{:S(2)}) copy-start(bf16[8,272,128]{2,1,0:T(8,128)(2,1)S(1)} %collective-permute-done.7.refs_2_) | copy-start | bytes 1671172
  54.2 13.4 %collective-permute-start.9 = (bf16[4,272,128]{2,1,0:T(8,128)(2,1)S(1)}, bf16[4,272,128]{2,1,0:T(8,128)(2,1)S(1)}, u32[]{:S(2)}, u32[]{:S(2)}) collective-permute-start(bf16[4,272,128]{2,1,0:T(8,128)(2,1)S(1)} %slice.193), channel_id=1, source_target_pairs={{0,192},{8,200},{16,208},{24,216},{32,224},{40,232},{48,240},{56,2... | collective-permute-start | bytes 835592 | tf_op jit(solution)/shard_map/ppermute | solution.py:257
  57.7 11.6 %copy-start.1 = (bf16[8,272,128]{2,1,0:T(8,128)(2,1)}, bf16[8,272,128]{2,1,0:T(8,128)(2,1)S(1)}, u32[]{:S(2)}) copy-start(bf16[8,272,128]{2,1,0:T(8,128)(2,1)S(1)} %collective-permute-done.6.refs_1_) | copy-start | bytes 1671172
  57.7 9.9 %collective-permute-start.8 = (bf16[4,272,128]{2,1,0:T(8,128)(2,1)S(1)}, bf16[4,272,128]{2,1,0:T(8,128)(2,1)S(1)}, u32[]{:S(2)}, u32[]{:S(2)}) collective-permute-start(bf16[4,272,128]{2,1,0:T(8,128)(2,1)S(1)} %slice.192), channel_id=1, source_target_pairs={{0,64},{8,72},{16,80},{24,88},{32,96},{40,104},{48,112},{56,120},{... | collective-permute-start | bytes 835592 | tf_op jit(solution)/shard_map/ppermute | solution.py:257
  60.9 6.7 %collective-permute-start.19 = (bf16[4,256,128]{2,1,0:T(8,128)(2,1)}, bf16[4,256,128]{2,1,0:T(8,128)(2,1)}, u32[]{:S(2)}, u32[]{:S(2)}) collective-permute-start(bf16[4,256,128]{2,1,0:T(8,128)(2,1)} %collective-permute-done.18.refs_11_), channel_id=1, source_target_pairs={{0,56},{8,0},{16,8},{24,16},{32,24},{40,32},{48,40},{56,48},{64,12... | collective-permute-start | bytes 786440 | tf_op jit(solution)/shard_map/ppermute | solution.py:257
  61.4 7.9 %collective-permute-start.16 = (bf16[4,256,128]{2,1,0:T(8,128)(2,1)}, bf16[4,256,128]{2,1,0:T(8,128)(2,1)}, u32[]{:S(2)}, u32[]{:S(2)}) collective-permute-start(bf16[4,256,128]{2,1,0:T(8,128)(2,1)} %collective-permute-done.15.refs_8_), channel_id=1, source_target_pairs={{0,8},{8,16},{16,24},{24,32},{32,40},{40,48},{48,56},{56,0},{64,72... | collective-permute-start | bytes 786440 | tf_op jit(solution)/shard_map/ppermute | solution.py:257
  67.6 1.7 %copy-start.7 = (bf16[4,272,128]{2,1,0:T(8,128)(2,1)}, bf16[4,272,128]{2,1,0:T(8,128)(2,1)S(1)}, u32[]{:S(2)}) copy-start(bf16[4,272,128]{2,1,0:T(8,128)(2,1)S(1)} %collective-permute-done.9.refs_4_) | copy-start | bytes 835588
  67.6 1.7 %copy-start.8 = (bf16[4,272,128]{2,1,0:T(8,128)(2,1)}, bf16[4,272,128]{2,1,0:T(8,128)(2,1)S(1)}, u32[]{:S(2)}) copy-start(bf16[4,272,128]{2,1,0:T(8,128)(2,1)S(1)} %collective-permute-done.8.refs_3_) | copy-start | bytes 835588
  89.0 3.1 %copy-start.4 = (bf16[8,256,128]{2,1,0:T(8,128)(2,1)S(1)}, bf16[8,256,128]{2,1,0:T(8,128)(2,1)}, u32[]{:S(2)}) copy-start(bf16[8,256,128]{2,1,0:T(8,128)(2,1)} %get-tuple-element.25) | copy-start | bytes 1572868
  89.0 3.1 %copy-start.5 = (bf16[8,256,128]{2,1,0:T(8,128)(2,1)S(1)}, bf16[8,256,128]{2,1,0:T(8,128)(2,1)}, u32[]{:S(2)}) copy-start(bf16[8,256,128]{2,1,0:T(8,128)(2,1)} %get-tuple-element.27) | copy-start | bytes 1572868
  89.0 5.4 %copy-start.19 = (bf16[4,256,128]{2,1,0:T(8,128)(2,1)S(1)}, bf16[4,256,128]{2,1,0:T(8,128)(2,1)}, u32[]{:S(2)}) copy-start(bf16[4,256,128]{2,1,0:T(8,128)(2,1)} %get-tuple-element.33) | copy-start | bytes 786436
  89.0 5.7 %copy-start.18 = (bf16[4,256,128]{2,1,0:T(8,128)(2,1)S(1)}, bf16[4,256,128]{2,1,0:T(8,128)(2,1)}, u32[]{:S(2)}) copy-start(bf16[4,256,128]{2,1,0:T(8,128)(2,1)} %get-tuple-element.36) | copy-start | bytes 786436
  89.1 16.3 %copy-start.16 = (bf16[4,256,128]{2,1,0:T(8,128)(2,1)S(1)}, bf16[4,256,128]{2,1,0:T(8,128)(2,1)}, u32[]{:S(2)}) copy-start(bf16[4,256,128]{2,1,0:T(8,128)(2,1)} %get-tuple-element.32) | copy-start | bytes 786436
  89.1 16.6 %copy-start.15 = (bf16[4,256,128]{2,1,0:T(8,128)(2,1)S(1)}, bf16[4,256,128]{2,1,0:T(8,128)(2,1)}, u32[]{:S(2)}) copy-start(bf16[4,256,128]{2,1,0:T(8,128)(2,1)} %get-tuple-element.35) | copy-start | bytes 786436
  89.1 23.0 %copy-start.14 = (bf16[4,256,128]{2,1,0:T(8,128)(2,1)S(1)}, bf16[4,256,128]{2,1,0:T(8,128)(2,1)}, u32[]{:S(2)}) copy-start(bf16[4,256,128]{2,1,0:T(8,128)(2,1)} %get-tuple-element.31) | copy-start | bytes 786436
  89.1 26.1 %copy-start.6 = (bf16[8,256,128]{2,1,0:T(8,128)(2,1)S(1)}, bf16[8,256,128]{2,1,0:T(8,128)(2,1)}, u32[]{:S(2)}) copy-start(bf16[8,256,128]{2,1,0:T(8,128)(2,1)} %get-tuple-element.24) | copy-start | bytes 1572868
  89.1 26.3 %copy-start.13 = (bf16[4,256,128]{2,1,0:T(8,128)(2,1)S(1)}, bf16[4,256,128]{2,1,0:T(8,128)(2,1)}, u32[]{:S(2)}) copy-start(bf16[4,256,128]{2,1,0:T(8,128)(2,1)} %get-tuple-element.34) | copy-start | bytes 786436
  89.1 40.0 %copy-start.10 = (bf16[4,256,128]{2,1,0:T(8,128)(2,1)S(1)}, bf16[4,256,128]{2,1,0:T(8,128)(2,1)}, u32[]{:S(2)}) copy-start(bf16[4,256,128]{2,1,0:T(8,128)(2,1)} %get-tuple-element.30) | copy-start | bytes 786436
  89.1 47.0 %copy-start.17 = (bf16[4,256,128]{2,1,0:T(8,128)(2,1)S(1)}, bf16[4,256,128]{2,1,0:T(8,128)(2,1)}, u32[]{:S(2)}) copy-start(bf16[4,256,128]{2,1,0:T(8,128)(2,1)} %get-tuple-element.29) | copy-start | bytes 786436
  89.1 11.7 %collective-permute-start.22 = (bf16[4,256,128]{2,1,0:T(8,128)(2,1)}, bf16[4,256,128]{2,1,0:T(8,128)(2,1)S(1)}, u32[]{:S(2)}, u32[]{:S(2)}) collective-permute-start(bf16[4,256,128]{2,1,0:T(8,128)(2,1)} %get-tuple-element.28), channel_id=1, source_target_pairs={{0,64},{8,72},{16,80},{24,88},{32,96},{40,104},{48,112},{56,120},{... | collective-permute-start | bytes 786440 | tf_op jit(solution)/shard_map/ppermute | solution.py:257
  92.2 9.4 %collective-permute-start.20 = (bf16[4,256,128]{2,1,0:T(8,128)(2,1)}, bf16[4,256,128]{2,1,0:T(8,128)(2,1)S(1)}, u32[]{:S(2)}, u32[]{:S(2)}) collective-permute-start(bf16[4,256,128]{2,1,0:T(8,128)(2,1)} %get-tuple-element.26), channel_id=1, source_target_pairs={{0,192},{8,200},{16,208},{24,216},{32,224},{40,232},{48,240},{56,2... | collective-permute-start | bytes 786440 | tf_op jit(solution)/shard_map/ppermute | solution.py:257
  94.5 10.9 %collective-permute-start.30 = (bf16[4,256,128]{2,1,0:T(8,128)(2,1)S(1)}, bf16[4,256,128]{2,1,0:T(8,128)(2,1)S(1)}, u32[]{:S(2)}, u32[]{:S(2)}) collective-permute-start(bf16[4,256,128]{2,1,0:T(8,128)(2,1)S(1)} %copy-done.19), channel_id=1, source_target_pairs={{0,56},{8,0},{16,8},{24,16},{32,24},{40,32},{48,40},{56,48},{64,12... | collective-permute-start | bytes 786440 | tf_op jit(solution)/shard_map/ppermute | solution.py:257
  94.7 11.0 %collective-permute-start.34 = (bf16[4,256,128]{2,1,0:T(8,128)(2,1)S(1)}, bf16[4,256,128]{2,1,0:T(8,128)(2,1)S(1)}, u32[]{:S(2)}, u32[]{:S(2)}) collective-permute-start(bf16[4,256,128]{2,1,0:T(8,128)(2,1)S(1)} %copy-done.18), channel_id=1, source_target_pairs={{0,8},{8,16},{16,24},{24,32},{32,40},{40,48},{48,56},{56,0},{64,72... | collective-permute-start | bytes 786440 | tf_op jit(solution)/shard_map/ppermute | solution.py:257
  100.9 14.2 %collective-permute-start.23 = (bf16[8,256,128]{2,1,0:T(8,128)(2,1)S(1)}, bf16[8,256,128]{2,1,0:T(8,128)(2,1)S(1)}, u32[]{:S(2)}, u32[]{:S(2)}) collective-permute-start(bf16[8,256,128]{2,1,0:T(8,128)(2,1)S(1)} %pad_maximum_fusion.1), channel_id=1, source_target_pairs={{0,64},{8,72},{16,80},{24,88},{32,96},{40,104},{48,112},{56,120},{... | collective-permute-start | bytes 1572872 | tf_op jit(solution)/shard_map/ppermute | solution.py:257
  101.7 13.4 %collective-permute-start.21 = (bf16[8,256,128]{2,1,0:T(8,128)(2,1)S(1)}, bf16[8,256,128]{2,1,0:T(8,128)(2,1)S(1)}, u32[]{:S(2)}, u32[]{:S(2)}) collective-permute-start(bf16[8,256,128]{2,1,0:T(8,128)(2,1)S(1)} %pad_maximum_fusion), channel_id=1, source_target_pairs={{0,192},{8,200},{16,208},{24,216},{32,224},{40,232},{48,240},{56,2... | collective-permute-start | bytes 1572872 | tf_op jit(solution)/shard_map/ppermute | solution.py:257
  105.4 6.7 %collective-permute-start.31 = (bf16[4,256,128]{2,1,0:T(8,128)(2,1)S(1)}, bf16[4,256,128]{2,1,0:T(8,128)(2,1)S(1)}, u32[]{:S(2)}, u32[]{:S(2)}) collective-permute-start(bf16[4,256,128]{2,1,0:T(8,128)(2,1)S(1)} %add_convert_fusion.4), channel_id=1, source_target_pairs={{0,56},{8,0},{16,8},{24,16},{32,24},{40,32},{48,40},{56,48},{64,12... | collective-permute-start | bytes 786440 | tf_op jit(solution)/shard_map/ppermute | solution.py:257
  105.8 9.6 %collective-permute-start.35 = (bf16[4,256,128]{2,1,0:T(8,128)(2,1)S(1)}, bf16[4,256,128]{2,1,0:T(8,128)(2,1)S(1)}, u32[]{:S(2)}, u32[]{:S(2)}) collective-permute-start(bf16[4,256,128]{2,1,0:T(8,128)(2,1)S(1)} %add_convert_fusion.1), channel_id=1, source_target_pairs={{0,8},{8,16},{16,24},{24,32},{32,40},{40,48},{48,56},{56,0},{64,72... | collective-permute-start | bytes 786440 | tf_op jit(solution)/shard_map/ppermute | solution.py:257
  112.2 17.0 %collective-permute-start.32 = (bf16[4,256,128]{2,1,0:T(8,128)(2,1)S(1)}, bf16[4,256,128]{2,1,0:T(8,128)(2,1)S(1)}, u32[]{:S(2)}, u32[]{:S(2)}) collective-permute-start(bf16[4,256,128]{2,1,0:T(8,128)(2,1)S(1)} %add_convert_fusion.3), channel_id=1, source_target_pairs={{0,56},{8,0},{16,8},{24,16},{32,24},{40,32},{48,40},{56,48},{64,12... | collective-permute-start | bytes 786440 | tf_op jit(solution)/shard_map/ppermute | solution.py:257
  115.3 10.7 %collective-permute-start.24 = (bf16[2,256,128]{2,1,0:T(8,128)(2,1)S(1)}, bf16[2,256,128]{2,1,0:T(8,128)(2,1)S(1)}, u32[]{:S(2)}, u32[]{:S(2)}) collective-permute-start(bf16[2,256,128]{2,1,0:T(8,128)(2,1)S(1)} %pad_maximum_fusion.4), channel_id=1, source_target_pairs={{0,48},{8,56},{16,0},{24,8},{32,16},{40,24},{48,32},{56,40},{64,11... | collective-permute-start | bytes 393224 | tf_op jit(solution)/shard_map/ppermute | solution.py:257
  115.4 18.9 %collective-permute-start.36 = (bf16[4,256,128]{2,1,0:T(8,128)(2,1)S(1)}, bf16[4,256,128]{2,1,0:T(8,128)(2,1)S(1)}, u32[]{:S(2)}, u32[]{:S(2)}) collective-permute-start(bf16[4,256,128]{2,1,0:T(8,128)(2,1)S(1)} %add_convert_fusion), channel_id=1, source_target_pairs={{0,8},{8,16},{16,24},{24,32},{32,40},{40,48},{48,56},{56,0},{64,72... | collective-permute-start | bytes 786440 | tf_op jit(solution)/shard_map/ppermute | solution.py:257
  126.1 7.8 %collective-permute-start.28 = (bf16[256,128]{1,0:T(8,128)(2,1)S(1)}, bf16[256,128]{1,0:T(8,128)(2,1)S(1)}, u32[]{:S(2)}, u32[]{:S(2)}) collective-permute-start(bf16[256,128]{1,0:T(8,128)(2,1)S(1)} %get-tuple-element.41), channel_id=1, source_target_pairs={{0,16},{8,24},{16,32},{24,40},{32,48},{40,56},{48,0},{56,8},{64,80... | collective-permute-start | bytes 196616 | tf_op jit(solution)/shard_map/ppermute | solution.py:257
  129.2 6.9 %collective-permute-start.33 = (bf16[4,256,128]{2,1,0:T(8,128)(2,1)S(1)}, bf16[4,256,128]{2,1,0:T(8,128)(2,1)S(1)}, u32[]{:S(2)}, u32[]{:S(2)}) collective-permute-start(bf16[4,256,128]{2,1,0:T(8,128)(2,1)S(1)} %add_convert_fusion.2), channel_id=1, source_target_pairs={{0,56},{8,0},{16,8},{24,16},{32,24},{40,32},{48,40},{56,48},{64,12... | collective-permute-start | bytes 786440 | tf_op jit(solution)/shard_map/ppermute | solution.py:257
  129.3 7.8 %collective-permute-start.25 = (bf16[256,128]{1,0:T(8,128)(2,1)S(1)}, bf16[256,128]{1,0:T(8,128)(2,1)S(1)}, u32[]{:S(2)}, u32[]{:S(2)}) collective-permute-start(bf16[256,128]{1,0:T(8,128)(2,1)S(1)} %get-tuple-element.39), channel_id=1, source_target_pairs={{0,56},{8,0},{16,8},{24,16},{32,24},{40,32},{48,40},{56,48},{64,12... | collective-permute-start | bytes 196616 | tf_op jit(solution)/shard_map/ppermute | solution.py:257
  131.0 7.3 %collective-permute-start.26 = (bf16[256,128]{1,0:T(8,128)(2,1)S(1)}, bf16[256,128]{1,0:T(8,128)(2,1)S(1)}, u32[]{:S(2)}, u32[]{:S(2)}) collective-permute-start(bf16[256,128]{1,0:T(8,128)(2,1)S(1)} %get-tuple-element.40), channel_id=1, source_target_pairs={{0,48},{8,56},{16,0},{24,8},{32,16},{40,24},{48,32},{56,40},{64,11... | collective-permute-start | bytes 196616 | tf_op jit(solution)/shard_map/ppermute | solution.py:257
  133.9 6.5 %collective-permute-start.27 = (bf16[256,128]{1,0:T(8,128)(2,1)S(1)}, bf16[256,128]{1,0:T(8,128)(2,1)S(1)}, u32[]{:S(2)}, u32[]{:S(2)}) collective-permute-start(bf16[256,128]{1,0:T(8,128)(2,1)S(1)} %get-tuple-element.42), channel_id=1, source_target_pairs={{0,16},{8,24},{16,32},{24,40},{32,48},{40,56},{48,0},{56,8},{64,80... | collective-permute-start | bytes 196616 | tf_op jit(solution)/shard_map/ppermute | solution.py:257
  134.4 6.3 %collective-permute-start.29 = (bf16[256,128]{1,0:T(8,128)(2,1)S(1)}, bf16[256,128]{1,0:T(8,128)(2,1)S(1)}, u32[]{:S(2)}, u32[]{:S(2)}) collective-permute-start(bf16[256,128]{1,0:T(8,128)(2,1)S(1)} %fusion.3), channel_id=1, source_target_pairs={{0,8},{8,16},{16,24},{24,32},{32,40},{40,48},{48,56},{56,0},{64,72... | collective-permute-start | bytes 196616 | tf_op jit(solution)/shard_map/ppermute | solution.py:257
  136.2 4.5 %collective-permute-start.37 = (bf16[256,128]{1,0:T(8,128)(2,1)S(1)}, bf16[256,128]{1,0:T(8,128)(2,1)S(1)}, u32[]{:S(2)}, u32[]{:S(2)}) collective-permute-start(bf16[256,128]{1,0:T(8,128)(2,1)S(1)} %get-tuple-element.45), channel_id=1, source_target_pairs={{0,192},{8,200},{16,208},{24,216},{32,224},{40,232},{48,240},{56,2... | collective-permute-start | bytes 196616 | tf_op jit(solution)/shard_map/ppermute | solution.py:257
  137.1 5.5 %collective-permute-start.39 = (bf16[256,128]{1,0:T(8,128)(2,1)S(1)}, bf16[256,128]{1,0:T(8,128)(2,1)S(1)}, u32[]{:S(2)}, u32[]{:S(2)}) collective-permute-start(bf16[256,128]{1,0:T(8,128)(2,1)S(1)} %get-tuple-element.46), channel_id=1, source_target_pairs={{0,64},{8,72},{16,80},{24,88},{32,96},{40,104},{48,112},{56,120},{... | collective-permute-start | bytes 196616 | tf_op jit(solution)/shard_map/ppermute | solution.py:257
  138.3 5.8 %collective-permute-start.38 = (bf16[256,128]{1,0:T(8,128)(2,1)S(1)}, bf16[256,128]{1,0:T(8,128)(2,1)S(1)}, u32[]{:S(2)}, u32[]{:S(2)}) collective-permute-start(bf16[256,128]{1,0:T(8,128)(2,1)S(1)} %get-tuple-element.47), channel_id=1, source_target_pairs={{0,128},{8,136},{16,144},{24,152},{32,160},{40,168},{48,176},{56,1... | collective-permute-start | bytes 196616 | tf_op jit(solution)/shard_map/ppermute | solution.py:257
Sparse Core Ops, SparseCore 0:
  89.3 43.8 reduce-scatter.1

commit v2 on v1

--- a/solution.py
+++ b/solution.py
@@ -278,7 +278,8 @@
     )(parents, lengths, keys, values)
 
     a1, a7, a2, a6 = (send(pack_a, 0, s) for s in (1, -1, 2, -2))
-    b1, b3, b2 = (send(pack_b, s, 0) for s in (1, -1, 2))
+    b1, b3 = send(pack_b, 1, 0), send(pack_b, -1, 0)
+    b2 = send(b1, 1, 0)
     near_b = jnp.stack([pack_b, b1, b2, b3])
     a34 = send(jnp.stack([a1, a2]), 0, 2)
     a5 = send(a7, 0, -2)

time: 152 us -> 148 us (0.974)
  waiting for transfers between devices: 52.9 us -> 49.2 us
    ppermute x40, waiting for transfers between devices: 52.9 us -> 49.2 us  [send(): return lax.ppermute(array, 'dp', pairs)]
  transfers between devices with their start and end apart: 41 -> 41, of which waited for: 19 -> 18; matrix products, arithmetic and copies ran while one was open for 3% -> 3% of each run, Pallas kernels for 0% -> 0%
where the time goes in v2:
time: 148 us
  starting transfers between devices  58.1 us (39%)
  waiting for transfers between devices  49.2 us (33%)
  Pallas kernels  21.3 us (14%)
  between operations  14.5 us (10%)
  other arithmetic  3.22 us (2%)
    ppermute x40, starting transfers between devices, send(): return lax.ppermute(array, 'dp', pairs)  58 us
    ppermute x40, waiting for transfers between devices, send(): return lax.ppermute(array, 'dp', pairs)  49.2 us
    pallas_call x1, Pallas kernels, main_call(): pl.pallas_call(functools.partial(main_kernel, node_count, nz), in_specs=[...  19.7 us
  transfers between devices with their start and end apart: 41, of which 18 were waited for; matrix products, arithmetic and copies ran while one was open for 3% of the time, Pallas kernels for 0%

profile of v2, /device:TPU:16, one launch (start us, length us, event | category | flops | bytes accessed | tf_op | source)
XLA Modules:
  0.0 147.6 jit_solution(6418242610193952018)
XLA Ops:
  7.2 1.6 %pack.1 = (bf16[272,128]{1,0:T(8,128)(2,1)}, bf16[256,128]{1,0:T(8,128)(2,1)}) custom-call(s32[6]{0:T(128)} %parents.3, s32[6]{0:T(128)} %lengths.3, bf16[768,256]{1,0:T(8,128)(2,1)} %k_hbm.1, bf16[768,256]{1,0:T(8,128)(2,1)} %v_hbm.1), custom_call_target="tpu_custom_call" | custom-call | tf_op jit(solution)/shard_map/pack/pallas_call | solution.py:265
  8.8 2.8 %collective-permute-start.12 = (bf16[256,128]{1,0:T(8,128)(2,1)}, bf16[256,128]{1,0:T(8,128)(2,1)S(1)}, u32[]{:S(2)}, u32[]{:S(2)}) collective-permute-start(bf16[256,128]{1,0:T(8,128)(2,1)} %get-tuple-element.22), channel_id=1, source_target_pairs={{0,192},{8,200},{16,208},{24,216},{32,224},{40,232},{48,240},{56,2... | collective-permute-start | bytes 196616 | tf_op jit(solution)/shard_map/ppermute | solution.py:257
  11.5 6.3 %collective-permute-start.5 = (bf16[272,128]{1,0:T(8,128)(2,1)}, bf16[272,128]{1,0:T(8,128)(2,1)S(1)}, u32[]{:S(2)}, u32[]{:S(2)}) collective-permute-start(bf16[272,128]{1,0:T(8,128)(2,1)} %get-tuple-element.21), channel_id=1, source_target_pairs={{0,48},{8,56},{16,0},{24,8},{32,16},{40,24},{48,32},{56,40},{64,11... | collective-permute-start | bytes 208904 | tf_op jit(solution)/shard_map/ppermute | solution.py:257
  17.8 1.0 collective-permute-start
  18.9 0.9 bitcast_dynamic-update-slice_fusion.3
  19.8 3.3 %collective-permute-start.3 = (bf16[272,128]{1,0:T(8,128)(2,1)}, bf16[272,128]{1,0:T(8,128)(2,1)S(1)}, u32[]{:S(2)}, u32[]{:S(2)}) collective-permute-start(bf16[272,128]{1,0:T(8,128)(2,1)} %get-tuple-element.21), channel_id=1, source_target_pairs={{0,56},{8,0},{16,8},{24,16},{32,24},{40,32},{48,40},{56,48},{64,12... | collective-permute-start | bytes 208904 | tf_op jit(solution)/shard_map/ppermute | solution.py:257
  23.1 2.1 %collective-permute-done.1 = bf16[272,128]{1,0:T(8,128)(2,1)S(1)} collective-permute-done((bf16[272,128]{1,0:T(8,128)(2,1)}, bf16[272,128]{1,0:T(8,128)(2,1)S(1)}, u32[]{:S(2)}, u32[]{:S(2)}) %collective-permute-start.1) | collective-permute-done | bytes 69664 | tf_op jit(solution)/shard_map/ppermute | solution.py:257
  25.2 0.2 collective-permute-start.11
  25.4 0.6 collective-permute-done
  26.1 0.1 collective-permute-start.2
  26.2 4.1 %collective-permute-start.4 = (bf16[272,128]{1,0:T(8,128)(2,1)S(1)}, bf16[272,128]{1,0:T(8,128)(2,1)S(1)}, u32[]{:S(2)}, u32[]{:S(2)}) collective-permute-start(bf16[272,128]{1,0:T(8,128)(2,1)S(1)} %collective-permute-done.3), channel_id=1, source_target_pairs={{0,48},{8,56},{16,0},{24,8},{32,16},{40,24},{48,32},{56,40},{64,11... | collective-permute-start | bytes 208904 | tf_op jit(solution)/shard_map/ppermute | solution.py:257
  30.3 0.4 collective-permute-done.11
  30.7 0.9 pad_maximum_fusion.2.refs_5_
  31.6 1.6 %collective-permute-start.13 = (bf16[4,256,128]{2,1,0:T(8,128)(2,1)S(1)}, bf16[4,256,128]{2,1,0:T(8,128)(2,1)S(1)}, u32[]{:S(2)}, u32[]{:S(2)}) collective-permute-start(bf16[4,256,128]{2,1,0:T(8,128)(2,1)S(1)} %pad_maximum_fusion.2.refs_5_), channel_id=1, source_target_pairs={{0,8},{8,16},{16,24},{24,32},{32,40},{40,48},{48,56},{56,0},{64,72... | collective-permute-start | bytes 786440 | tf_op jit(solution)/shard_map/ppermute | solution.py:257
  33.2 2.9 %collective-permute-done.2 = bf16[2,272,128]{2,1,0:T(8,128)(2,1)S(1)} collective-permute-done((bf16[2,272,128]{2,1,0:T(8,128)(2,1)S(1)}, bf16[2,272,128]{2,1,0:T(8,128)(2,1)S(1)}, u32[]{:S(2)}, u32[]{:S(2)}) %collective-permute-start.2) | collective-permute-done | bytes 139296 | tf_op jit(solution)/shard_map/ppermute | solution.py:257
  36.2 2.9 %collective-permute-start.7 = (bf16[8,272,128]{2,1,0:T(8,128)(2,1)S(1)}, bf16[8,272,128]{2,1,0:T(8,128)(2,1)S(1)}, u32[]{:S(2)}, u32[]{:S(2)}) collective-permute-start(bf16[8,272,128]{2,1,0:T(8,128)(2,1)S(1)} %bitcast_dynamic-update-slice_fusion.refs_0_), channel_id=1, source_target_pairs={{0,192},{8,200},{16,208},{24,216},{32,224},{40,232},{48,240},{56,2... | collective-permute-start | bytes 1671176 | tf_op jit(solution)/shard_map/ppermute | solution.py:257
  39.1 0.4 collective-permute-start.17
  39.5 1.6 %collective-permute-done.13.refs_6_ = bf16[4,256,128]{2,1,0:T(8,128)(2,1)S(1)} collective-permute-done((bf16[4,256,128]{2,1,0:T(8,128)(2,1)S(1)}, bf16[4,256,128]{2,1,0:T(8,128)(2,1)S(1)}, u32[]{:S(2)}, u32[]{:S(2)}) %collective-permute-start.13) | collective-permute-done | bytes 262176 | tf_op jit(solution)/shard_map/ppermute | solution.py:257
  41.0 0.1 collective-permute-start.14
  41.1 6.8 %collective-permute-done.17.refs_12_ = bf16[4,256,128]{2,1,0:T(8,128)(2,1)S(1)} collective-permute-done((bf16[4,256,128]{2,1,0:T(8,128)(2,1)S(1)}, bf16[4,256,128]{2,1,0:T(8,128)(2,1)S(1)}, u32[]{:S(2)}, u32[]{:S(2)}) %collective-permute-start.17) | collective-permute-done | bytes 262176 | tf_op jit(solution)/shard_map/ppermute | solution.py:257
  47.9 1.4 collective-permute-done.14.refs_7_
  49.4 0.6 collective-permute-start.15
  50.0 2.8 %collective-permute-start.9 = (bf16[4,272,128]{2,1,0:T(8,128)(2,1)S(1)}, bf16[4,272,128]{2,1,0:T(8,128)(2,1)S(1)}, u32[]{:S(2)}, u32[]{:S(2)}) collective-permute-start(bf16[4,272,128]{2,1,0:T(8,128)(2,1)S(1)} %slice.193), channel_id=1, source_target_pairs={{0,192},{8,200},{16,208},{24,216},{32,224},{40,232},{48,240},{56,2... | collective-permute-start | bytes 835592 | tf_op jit(solution)/shard_map/ppermute | solution.py:257
  52.8 0.1 collective-permute-start.8
  52.9 3.9 %collective-permute-done.18.refs_11_ = bf16[4,256,128]{2,1,0:T(8,128)(2,1)} collective-permute-done((bf16[4,256,128]{2,1,0:T(8,128)(2,1)S(1)}, bf16[4,256,128]{2,1,0:T(8,128)(2,1)}, u32[]{:S(2)}, u32[]{:S(2)}) %collective-permute-start.18) | collective-permute-done | bytes 262176 | tf_op jit(solution)/shard_map/ppermute | solution.py:257
  56.8 0.2 collective-permute-done.15.refs_8_
  57.0 1.8 %collective-permute-start.16 = (bf16[4,256,128]{2,1,0:T(8,128)(2,1)}, bf16[4,256,128]{2,1,0:T(8,128)(2,1)}, u32[]{:S(2)}, u32[]{:S(2)}) collective-permute-start(bf16[4,256,128]{2,1,0:T(8,128)(2,1)} %collective-permute-done.15.refs_8_), channel_id=1, source_target_pairs={{0,8},{8,16},{16,24},{24,32},{32,40},{40,48},{48,56},{56,0},{64,72... | collective-permute-start | bytes 786440 | tf_op jit(solution)/shard_map/ppermute | solution.py:257
  58.9 0.6 pad_add_fusion.spot
  59.4 4.1 %collective-permute-done.19.refs_10_ = bf16[4,256,128]{2,1,0:T(8,128)(2,1)} collective-permute-done((bf16[4,256,128]{2,1,0:T(8,128)(2,1)}, bf16[4,256,128]{2,1,0:T(8,128)(2,1)}, u32[]{:S(2)}, u32[]{:S(2)}) %collective-permute-start.19) | collective-permute-done | bytes 262176 | tf_op jit(solution)/shard_map/ppermute | solution.py:257
  63.5 1.4 collective-permute-done.16.refs_9_
  65.0 19.7 %attention.1 = (bf16[768,256]{1,0:T(8,128)(2,1)}, bf16[768,256]{1,0:T(8,128)(2,1)}, bf16[4608,768]{1,0:T(8,128)(2,1)}, bf16[8,256,128]{2,1,0:T(8,128)(2,1)}, bf1...) custom-call(s32[6]{0:T(128)} %parents.3, ...), custom_call_target="tpu_custom_call" | custom-call | tf_op jit(solution)/shard_map/attention/pallas_call | solution.py:207
  84.8 0.8 collective-permute-start.22
  85.6 0.1 copy-done.4
  85.8 0.1 copy-done.5
  85.9 4.1 %collective-permute-start.20 = (bf16[4,256,128]{2,1,0:T(8,128)(2,1)}, bf16[4,256,128]{2,1,0:T(8,128)(2,1)S(1)}, u32[]{:S(2)}, u32[]{:S(2)}) collective-permute-start(bf16[4,256,128]{2,1,0:T(8,128)(2,1)} %get-tuple-element.26), channel_id=1, source_target_pairs={{0,192},{8,200},{16,208},{24,216},{32,224},{40,232},{48,240},{56,2... | collective-permute-start | bytes 786440 | tf_op jit(solution)/shard_map/ppermute | solution.py:257
  90.0 0.7 collective-permute-start.30
  90.7 1.3 collective-permute-start.34
  92.0 3.6 %collective-permute-done.22 = bf16[4,256,128]{2,1,0:T(8,128)(2,1)S(1)} collective-permute-done((bf16[4,256,128]{2,1,0:T(8,128)(2,1)}, bf16[4,256,128]{2,1,0:T(8,128)(2,1)S(1)}, u32[]{:S(2)}, u32[]{:S(2)}) %collective-permute-start.22) | collective-permute-done | bytes 262176 | tf_op jit(solution)/shard_map/ppermute | solution.py:257
  95.7 0.1 collective-permute-start.23
  95.8 1.1 collective-permute-done.20
  97.1 3.7 %collective-permute-start.21 = (bf16[8,256,128]{2,1,0:T(8,128)(2,1)S(1)}, bf16[8,256,128]{2,1,0:T(8,128)(2,1)S(1)}, u32[]{:S(2)}, u32[]{:S(2)}) collective-permute-start(bf16[8,256,128]{2,1,0:T(8,128)(2,1)S(1)} %pad_maximum_fusion), channel_id=1, source_target_pairs={{0,192},{8,200},{16,208},{24,216},{32,224},{40,232},{48,240},{56,2... | collective-permute-start | bytes 1572872 | tf_op jit(solution)/shard_map/ppermute | solution.py:257
  100.8 0.8 collective-permute-start.31
  101.7 1.6 %collective-permute-start.35 = (bf16[4,256,128]{2,1,0:T(8,128)(2,1)S(1)}, bf16[4,256,128]{2,1,0:T(8,128)(2,1)S(1)}, u32[]{:S(2)}, u32[]{:S(2)}) collective-permute-start(bf16[4,256,128]{2,1,0:T(8,128)(2,1)S(1)} %add_convert_fusion.1), channel_id=1, source_target_pairs={{0,8},{8,16},{16,24},{24,32},{32,40},{40,48},{48,56},{56,0},{64,72... | collective-permute-start | bytes 786440 | tf_op jit(solution)/shard_map/ppermute | solution.py:257
  103.3 6.7 %collective-permute-done.31 = bf16[4,256,128]{2,1,0:T(8,128)(2,1)S(1)} collective-permute-done((bf16[4,256,128]{2,1,0:T(8,128)(2,1)S(1)}, bf16[4,256,128]{2,1,0:T(8,128)(2,1)S(1)}, u32[]{:S(2)}, u32[]{:S(2)}) %collective-permute-start.31) | collective-permute-done | bytes 262176 | tf_op jit(solution)/shard_map/ppermute | solution.py:257
  110.1 2.2 %collective-permute-start.32 = (bf16[4,256,128]{2,1,0:T(8,128)(2,1)S(1)}, bf16[4,256,128]{2,1,0:T(8,128)(2,1)S(1)}, u32[]{:S(2)}, u32[]{:S(2)}) collective-permute-start(bf16[4,256,128]{2,1,0:T(8,128)(2,1)S(1)} %add_convert_fusion.3), channel_id=1, source_target_pairs={{0,56},{8,0},{16,8},{24,16},{32,24},{40,32},{48,40},{56,48},{64,12... | collective-permute-start | bytes 786440 | tf_op jit(solution)/shard_map/ppermute | solution.py:257
  112.4 0.1 collective-permute-start.24
  112.5 0.1 add_convert_fusion
  112.5 1.5 %collective-permute-start.36 = (bf16[4,256,128]{2,1,0:T(8,128)(2,1)S(1)}, bf16[4,256,128]{2,1,0:T(8,128)(2,1)S(1)}, u32[]{:S(2)}, u32[]{:S(2)}) collective-permute-start(bf16[4,256,128]{2,1,0:T(8,128)(2,1)S(1)} %add_convert_fusion), channel_id=1, source_target_pairs={{0,8},{8,16},{16,24},{24,32},{32,40},{40,48},{48,56},{56,0},{64,72... | collective-permute-start | bytes 786440 | tf_op jit(solution)/shard_map/ppermute | solution.py:257
  114.1 9.0 %collective-permute-done.24 = bf16[2,256,128]{2,1,0:T(8,128)(2,1)S(1)} collective-permute-done((bf16[2,256,128]{2,1,0:T(8,128)(2,1)S(1)}, bf16[2,256,128]{2,1,0:T(8,128)(2,1)S(1)}, u32[]{:S(2)}, u32[]{:S(2)}) %collective-permute-start.24) | collective-permute-done | bytes 131104 | tf_op jit(solution)/shard_map/ppermute | solution.py:257
  123.1 0.1 fusion.16
  123.2 1.6 %collective-permute-start.28 = (bf16[256,128]{1,0:T(8,128)(2,1)S(1)}, bf16[256,128]{1,0:T(8,128)(2,1)S(1)}, u32[]{:S(2)}, u32[]{:S(2)}) collective-permute-start(bf16[256,128]{1,0:T(8,128)(2,1)S(1)} %get-tuple-element.41), channel_id=1, source_target_pairs={{0,16},{8,24},{16,32},{24,40},{32,48},{40,56},{48,0},{56,8},{64,80... | collective-permute-start | bytes 196616 | tf_op jit(solution)/shard_map/ppermute | solution.py:257
  125.0 2.0 %collective-permute-start.33 = (bf16[4,256,128]{2,1,0:T(8,128)(2,1)S(1)}, bf16[4,256,128]{2,1,0:T(8,128)(2,1)S(1)}, u32[]{:S(2)}, u32[]{:S(2)}) collective-permute-start(bf16[4,256,128]{2,1,0:T(8,128)(2,1)S(1)} %add_convert_fusion.2), channel_id=1, source_target_pairs={{0,56},{8,0},{16,8},{24,16},{32,24},{40,32},{48,40},{56,48},{64,12... | collective-permute-start | bytes 786440 | tf_op jit(solution)/shard_map/ppermute | solution.py:257
  127.0 1.2 collective-permute-start.25
  128.2 1.8 %collective-permute-start.26 = (bf16[256,128]{1,0:T(8,128)(2,1)S(1)}, bf16[256,128]{1,0:T(8,128)(2,1)S(1)}, u32[]{:S(2)}, u32[]{:S(2)}) collective-permute-start(bf16[256,128]{1,0:T(8,128)(2,1)S(1)} %get-tuple-element.40), channel_id=1, source_target_pairs={{0,48},{8,56},{16,0},{24,8},{32,16},{40,24},{48,32},{56,40},{64,11... | collective-permute-start | bytes 196616 | tf_op jit(solution)/shard_map/ppermute | solution.py:257
  130.0 1.1 collective-permute-start.27
  131.2 0.9 collective-permute-start.29
  132.1 0.1 fusion.13
  132.2 1.6 %collective-permute-start.37 = (bf16[256,128]{1,0:T(8,128)(2,1)S(1)}, bf16[256,128]{1,0:T(8,128)(2,1)S(1)}, u32[]{:S(2)}, u32[]{:S(2)}) collective-permute-start(bf16[256,128]{1,0:T(8,128)(2,1)S(1)} %get-tuple-element.45), channel_id=1, source_target_pairs={{0,192},{8,200},{16,208},{24,216},{32,224},{40,232},{48,240},{56,2... | collective-permute-start | bytes 196616 | tf_op jit(solution)/shard_map/ppermute | solution.py:257
  133.7 0.5 collective-permute-start.39
  134.3 2.3 %collective-permute-start.38 = (bf16[256,128]{1,0:T(8,128)(2,1)S(1)}, bf16[256,128]{1,0:T(8,128)(2,1)S(1)}, u32[]{:S(2)}, u32[]{:S(2)}) collective-permute-start(bf16[256,128]{1,0:T(8,128)(2,1)S(1)} %get-tuple-element.47), channel_id=1, source_target_pairs={{0,128},{8,136},{16,144},{24,152},{32,160},{40,168},{48,176},{56,1... | collective-permute-start | bytes 196616 | tf_op jit(solution)/shard_map/ppermute | solution.py:257
  136.6 1.2 collective-permute-done.29
  137.9 1.3 collective-permute-done.39
  139.2 0.8 collective-permute-done.38
  140.1 0.7 maximum_dynamic-update-slice_fusion
  (94 shorter events, 1.2 us)
Async XLA Ops:
  7.2 133.6 %reduce-scatter.2.cloned.1.call-start = ((), (), s32[]{:S(2)}) async-start(), calls=%async_computation.1 | async-start | bytes 7962624 | tf_op jit(solution)/shard_map/reduce_scatter | solution.py:300
  8.8 21.6 %collective-permute-start.12 = (bf16[256,128]{1,0:T(8,128)(2,1)}, bf16[256,128]{1,0:T(8,128)(2,1)S(1)}, u32[]{:S(2)}, u32[]{:S(2)}) collective-permute-start(bf16[256,128]{1,0:T(8,128)(2,1)} %get-tuple-element.22), channel_id=1, source_target_pairs={{0,192},{8,200},{16,208},{24,216},{32,224},{40,232},{48,240},{56,2... | collective-permute-start | bytes 196616 | tf_op jit(solution)/shard_map/ppermute | solution.py:257
  11.5 8.3 %collective-permute-start.10 = (bf16[256,128]{1,0:T(8,128)(2,1)}, bf16[256,128]{1,0:T(8,128)(2,1)S(1)}, u32[]{:S(2)}, u32[]{:S(2)}) collective-permute-start(bf16[256,128]{1,0:T(8,128)(2,1)} %get-tuple-element.22), channel_id=1, source_target_pairs={{0,64},{8,72},{16,80},{24,88},{32,96},{40,104},{48,112},{56,120},{... | collective-permute-start | bytes 196616 | tf_op jit(solution)/shard_map/ppermute | solution.py:257
  11.5 24.6 %collective-permute-start.5 = (bf16[272,128]{1,0:T(8,128)(2,1)}, bf16[272,128]{1,0:T(8,128)(2,1)S(1)}, u32[]{:S(2)}, u32[]{:S(2)}) collective-permute-start(bf16[272,128]{1,0:T(8,128)(2,1)} %get-tuple-element.21), channel_id=1, source_target_pairs={{0,48},{8,56},{16,0},{24,8},{32,16},{40,24},{48,32},{56,40},{64,11... | collective-permute-start | bytes 208904 | tf_op jit(solution)/shard_map/ppermute | solution.py:257
  17.8 7.4 %collective-permute-start.1 = (bf16[272,128]{1,0:T(8,128)(2,1)}, bf16[272,128]{1,0:T(8,128)(2,1)S(1)}, u32[]{:S(2)}, u32[]{:S(2)}) collective-permute-start(bf16[272,128]{1,0:T(8,128)(2,1)} %get-tuple-element.21), channel_id=1, source_target_pairs={{0,16},{8,24},{16,32},{24,40},{32,48},{40,56},{48,0},{56,8},{64,80... | collective-permute-start | bytes 208904 | tf_op jit(solution)/shard_map/ppermute | solution.py:257
  17.8 8.2 %collective-permute-start = (bf16[272,128]{1,0:T(8,128)(2,1)}, bf16[272,128]{1,0:T(8,128)(2,1)S(1)}, u32[]{:S(2)}, u32[]{:S(2)}) collective-permute-start(bf16[272,128]{1,0:T(8,128)(2,1)} %get-tuple-element.21), channel_id=1, source_target_pairs={{0,8},{8,16},{16,24},{24,32},{32,40},{40,48},{48,56},{56,0},{64,72... | collective-permute-start | bytes 208904 | tf_op jit(solution)/shard_map/ppermute | solution.py:257
  19.8 6.4 %collective-permute-start.3 = (bf16[272,128]{1,0:T(8,128)(2,1)}, bf16[272,128]{1,0:T(8,128)(2,1)S(1)}, u32[]{:S(2)}, u32[]{:S(2)}) collective-permute-start(bf16[272,128]{1,0:T(8,128)(2,1)} %get-tuple-element.21), channel_id=1, source_target_pairs={{0,56},{8,0},{16,8},{24,16},{32,24},{40,32},{48,40},{56,48},{64,12... | collective-permute-start | bytes 208904 | tf_op jit(solution)/shard_map/ppermute | solution.py:257
  25.2 5.5 %collective-permute-start.11 = (bf16[256,128]{1,0:T(8,128)(2,1)S(1)}, bf16[256,128]{1,0:T(8,128)(2,1)S(1)}, u32[]{:S(2)}, u32[]{:S(2)}) collective-permute-start(bf16[256,128]{1,0:T(8,128)(2,1)S(1)} %collective-permute-done.10), channel_id=1, source_target_pairs={{0,64},{8,72},{16,80},{24,88},{32,96},{40,104},{48,112},{56,120},{... | collective-permute-start | bytes 196616 | tf_op jit(solution)/shard_map/ppermute | solution.py:257
  26.1 10.0 %collective-permute-start.2 = (bf16[2,272,128]{2,1,0:T(8,128)(2,1)S(1)}, bf16[2,272,128]{2,1,0:T(8,128)(2,1)S(1)}, u32[]{:S(2)}, u32[]{:S(2)}) collective-permute-start(bf16[2,272,128]{2,1,0:T(8,128)(2,1)S(1)} %pad_maximum_fusion.3), channel_id=1, source_target_pairs={{0,16},{8,24},{16,32},{24,40},{32,48},{40,56},{48,0},{56,8},{64,80... | collective-permute-start | bytes 417800 | tf_op jit(solution)/shard_map/ppermute | solution.py:257
  26.2 9.9 %collective-permute-start.4 = (bf16[272,128]{1,0:T(8,128)(2,1)S(1)}, bf16[272,128]{1,0:T(8,128)(2,1)S(1)}, u32[]{:S(2)}, u32[]{:S(2)}) collective-permute-start(bf16[272,128]{1,0:T(8,128)(2,1)S(1)} %collective-permute-done.3), channel_id=1, source_target_pairs={{0,48},{8,56},{16,0},{24,8},{32,16},{40,24},{48,32},{56,40},{64,11... | collective-permute-start | bytes 208904 | tf_op jit(solution)/shard_map/ppermute | solution.py:257
  31.6 33.4 %copy-start.2 = (bf16[4,256,128]{2,1,0:T(8,128)(2,1)}, bf16[4,256,128]{2,1,0:T(8,128)(2,1)S(1)}, u32[]{:S(2)}) copy-start(bf16[4,256,128]{2,1,0:T(8,128)(2,1)S(1)} %pad_maximum_fusion.2.refs_5_) | copy-start | bytes 786436
  31.6 9.4 %collective-permute-start.13 = (bf16[4,256,128]{2,1,0:T(8,128)(2,1)S(1)}, bf16[4,256,128]{2,1,0:T(8,128)(2,1)S(1)}, u32[]{:S(2)}, u32[]{:S(2)}) collective-permute-start(bf16[4,256,128]{2,1,0:T(8,128)(2,1)S(1)} %pad_maximum_fusion.2.refs_5_), channel_id=1, source_target_pairs={{0,8},{8,16},{16,24},{24,32},{32,40},{40,48},{48,56},{56,0},{64,72... | collective-permute-start | bytes 786440 | tf_op jit(solution)/shard_map/ppermute | solution.py:257
  36.2 28.7 %copy-start.3 = (bf16[8,272,128]{2,1,0:T(8,128)(2,1)}, bf16[8,272,128]{2,1,0:T(8,128)(2,1)S(1)}, u32[]{:S(2)}) copy-start(bf16[8,272,128]{2,1,0:T(8,128)(2,1)S(1)} %bitcast_dynamic-update-slice_fusion.refs_0_) | copy-start | bytes 1671172
  36.2 13.7 %collective-permute-start.7 = (bf16[8,272,128]{2,1,0:T(8,128)(2,1)S(1)}, bf16[8,272,128]{2,1,0:T(8,128)(2,1)S(1)}, u32[]{:S(2)}, u32[]{:S(2)}) collective-permute-start(bf16[8,272,128]{2,1,0:T(8,128)(2,1)S(1)} %bitcast_dynamic-update-slice_fusion.refs_0_), channel_id=1, source_target_pairs={{0,192},{8,200},{16,208},{24,216},{32,224},{40,232},{48,240},{56,2... | collective-permute-start | bytes 1671176 | tf_op jit(solution)/shard_map/ppermute | solution.py:257
  39.1 13.7 %collective-permute-start.6 = (bf16[8,272,128]{2,1,0:T(8,128)(2,1)S(1)}, bf16[8,272,128]{2,1,0:T(8,128)(2,1)S(1)}, u32[]{:S(2)}, u32[]{:S(2)}) collective-permute-start(bf16[8,272,128]{2,1,0:T(8,128)(2,1)S(1)} %bitcast_dynamic-update-slice_fusion.refs_0_), channel_id=1, source_target_pairs={{0,64},{8,72},{16,80},{24,88},{32,96},{40,104},{48,112},{56,120},{... | collective-permute-start | bytes 1671176 | tf_op jit(solution)/shard_map/ppermute | solution.py:257
  39.1 8.8 %collective-permute-start.17 = (bf16[4,256,128]{2,1,0:T(8,128)(2,1)S(1)}, bf16[4,256,128]{2,1,0:T(8,128)(2,1)S(1)}, u32[]{:S(2)}, u32[]{:S(2)}) collective-permute-start(bf16[4,256,128]{2,1,0:T(8,128)(2,1)S(1)} %pad_maximum_fusion.2.refs_5_), channel_id=1, source_target_pairs={{0,56},{8,0},{16,8},{24,16},{32,24},{40,32},{48,40},{56,48},{64,12... | collective-permute-start | bytes 786440 | tf_op jit(solution)/shard_map/ppermute | solution.py:257
  41.0 23.9 %copy-start.9 = (bf16[4,256,128]{2,1,0:T(8,128)(2,1)}, bf16[4,256,128]{2,1,0:T(8,128)(2,1)S(1)}, u32[]{:S(2)}) copy-start(bf16[4,256,128]{2,1,0:T(8,128)(2,1)S(1)} %collective-permute-done.13.refs_6_) | copy-start | bytes 786436
  41.0 8.3 %collective-permute-start.14 = (bf16[4,256,128]{2,1,0:T(8,128)(2,1)S(1)}, bf16[4,256,128]{2,1,0:T(8,128)(2,1)S(1)}, u32[]{:S(2)}, u32[]{:S(2)}) collective-permute-start(bf16[4,256,128]{2,1,0:T(8,128)(2,1)S(1)} %collective-permute-done.13.refs_6_), channel_id=1, source_target_pairs={{0,8},{8,16},{16,24},{24,32},{32,40},{40,48},{48,56},{56,0},{64,72... | collective-permute-start | bytes 786440 | tf_op jit(solution)/shard_map/ppermute | solution.py:257
  47.9 5.0 %copy-start.11 = (bf16[4,256,128]{2,1,0:T(8,128)(2,1)}, bf16[4,256,128]{2,1,0:T(8,128)(2,1)S(1)}, u32[]{:S(2)}) copy-start(bf16[4,256,128]{2,1,0:T(8,128)(2,1)S(1)} %collective-permute-done.17.refs_12_) | copy-start | bytes 786436
  47.9 8.9 %collective-permute-start.18 = (bf16[4,256,128]{2,1,0:T(8,128)(2,1)S(1)}, bf16[4,256,128]{2,1,0:T(8,128)(2,1)}, u32[]{:S(2)}, u32[]{:S(2)}) collective-permute-start(bf16[4,256,128]{2,1,0:T(8,128)(2,1)S(1)} %collective-permute-done.17.refs_12_), channel_id=1, source_target_pairs={{0,56},{8,0},{16,8},{24,16},{32,24},{40,32},{48,40},{56,48},{64,12... | collective-permute-start | bytes 786440 | tf_op jit(solution)/shard_map/ppermute | solution.py:257
  49.3 7.5 %copy-start.12 = (bf16[4,256,128]{2,1,0:T(8,128)(2,1)}, bf16[4,256,128]{2,1,0:T(8,128)(2,1)S(1)}, u32[]{:S(2)}) copy-start(bf16[4,256,128]{2,1,0:T(8,128)(2,1)S(1)} %collective-permute-done.14.refs_7_) | copy-start | bytes 786436
  49.4 7.7 %collective-permute-start.15 = (bf16[4,256,128]{2,1,0:T(8,128)(2,1)S(1)}, bf16[4,256,128]{2,1,0:T(8,128)(2,1)}, u32[]{:S(2)}, u32[]{:S(2)}) collective-permute-start(bf16[4,256,128]{2,1,0:T(8,128)(2,1)S(1)} %collective-permute-done.14.refs_7_), channel_id=1, source_target_pairs={{0,8},{8,16},{16,24},{24,32},{32,40},{40,48},{48,56},{56,0},{64,72... | collective-permute-start | bytes 786440 | tf_op jit(solution)/shard_map/ppermute | solution.py:257
  49.9 15.0 %copy-start = (bf16[8,272,128]{2,1,0:T(8,128)(2,1)}, bf16[8,272,128]{2,1,0:T(8,128)(2,1)S(1)}, u32[]{:S(2)}) copy-start(bf16[8,272,128]{2,1,0:T(8,128)(2,1)S(1)} %collective-permute-done.7.refs_2_) | copy-start | bytes 1671172
  50.0 13.5 %collective-permute-start.9 = (bf16[4,272,128]{2,1,0:T(8,128)(2,1)S(1)}, bf16[4,272,128]{2,1,0:T(8,128)(2,1)S(1)}, u32[]{:S(2)}, u32[]{:S(2)}) collective-permute-start(bf16[4,272,128]{2,1,0:T(8,128)(2,1)S(1)} %slice.193), channel_id=1, source_target_pairs={{0,192},{8,200},{16,208},{24,216},{32,224},{40,232},{48,240},{56,2... | collective-permute-start | bytes 835592 | tf_op jit(solution)/shard_map/ppermute | solution.py:257
  52.8 12.2 %copy-start.1 = (bf16[8,272,128]{2,1,0:T(8,128)(2,1)}, bf16[8,272,128]{2,1,0:T(8,128)(2,1)S(1)}, u32[]{:S(2)}) copy-start(bf16[8,272,128]{2,1,0:T(8,128)(2,1)S(1)} %collective-permute-done.6.refs_1_) | copy-start | bytes 1671172
  52.8 10.7 %collective-permute-start.8 = (bf16[4,272,128]{2,1,0:T(8,128)(2,1)S(1)}, bf16[4,272,128]{2,1,0:T(8,128)(2,1)S(1)}, u32[]{:S(2)}, u32[]{:S(2)}) collective-permute-start(bf16[4,272,128]{2,1,0:T(8,128)(2,1)S(1)} %slice.192), channel_id=1, source_target_pairs={{0,64},{8,72},{16,80},{24,88},{32,96},{40,104},{48,112},{56,120},{... | collective-permute-start | bytes 835592 | tf_op jit(solution)/shard_map/ppermute | solution.py:257
  56.8 6.7 %collective-permute-start.19 = (bf16[4,256,128]{2,1,0:T(8,128)(2,1)}, bf16[4,256,128]{2,1,0:T(8,128)(2,1)}, u32[]{:S(2)}, u32[]{:S(2)}) collective-permute-start(bf16[4,256,128]{2,1,0:T(8,128)(2,1)} %collective-permute-done.18.refs_11_), channel_id=1, source_target_pairs={{0,56},{8,0},{16,8},{24,16},{32,24},{40,32},{48,40},{56,48},{64,12... | collective-permute-start | bytes 786440 | tf_op jit(solution)/shard_map/ppermute | solution.py:257
  57.0 7.9 %collective-permute-start.16 = (bf16[4,256,128]{2,1,0:T(8,128)(2,1)}, bf16[4,256,128]{2,1,0:T(8,128)(2,1)}, u32[]{:S(2)}, u32[]{:S(2)}) collective-permute-start(bf16[4,256,128]{2,1,0:T(8,128)(2,1)} %collective-permute-done.15.refs_8_), channel_id=1, source_target_pairs={{0,8},{8,16},{16,24},{24,32},{32,40},{40,48},{48,56},{56,0},{64,72... | collective-permute-start | bytes 786440 | tf_op jit(solution)/shard_map/ppermute | solution.py:257
  63.5 1.5 copy-start.7
  63.5 1.5 copy-start.8
  84.7 1.0 copy-start.4
  84.7 1.2 copy-start.5
  84.7 5.3 %copy-start.19 = (bf16[4,256,128]{2,1,0:T(8,128)(2,1)S(1)}, bf16[4,256,128]{2,1,0:T(8,128)(2,1)}, u32[]{:S(2)}) copy-start(bf16[4,256,128]{2,1,0:T(8,128)(2,1)} %get-tuple-element.33) | copy-start | bytes 786436
  84.7 6.0 %copy-start.18 = (bf16[4,256,128]{2,1,0:T(8,128)(2,1)S(1)}, bf16[4,256,128]{2,1,0:T(8,128)(2,1)}, u32[]{:S(2)}) copy-start(bf16[4,256,128]{2,1,0:T(8,128)(2,1)} %get-tuple-element.36) | copy-start | bytes 786436
  84.7 16.0 %copy-start.16 = (bf16[4,256,128]{2,1,0:T(8,128)(2,1)S(1)}, bf16[4,256,128]{2,1,0:T(8,128)(2,1)}, u32[]{:S(2)}) copy-start(bf16[4,256,128]{2,1,0:T(8,128)(2,1)} %get-tuple-element.32) | copy-start | bytes 786436
  84.7 16.9 %copy-start.15 = (bf16[4,256,128]{2,1,0:T(8,128)(2,1)S(1)}, bf16[4,256,128]{2,1,0:T(8,128)(2,1)}, u32[]{:S(2)}) copy-start(bf16[4,256,128]{2,1,0:T(8,128)(2,1)} %get-tuple-element.35) | copy-start | bytes 786436
  84.8 25.2 %copy-start.14 = (bf16[4,256,128]{2,1,0:T(8,128)(2,1)S(1)}, bf16[4,256,128]{2,1,0:T(8,128)(2,1)}, u32[]{:S(2)}) copy-start(bf16[4,256,128]{2,1,0:T(8,128)(2,1)} %get-tuple-element.31) | copy-start | bytes 786436
  84.8 27.5 %copy-start.6 = (bf16[8,256,128]{2,1,0:T(8,128)(2,1)S(1)}, bf16[8,256,128]{2,1,0:T(8,128)(2,1)}, u32[]{:S(2)}) copy-start(bf16[8,256,128]{2,1,0:T(8,128)(2,1)} %get-tuple-element.24) | copy-start | bytes 1572868
  84.8 27.7 %copy-start.13 = (bf16[4,256,128]{2,1,0:T(8,128)(2,1)S(1)}, bf16[4,256,128]{2,1,0:T(8,128)(2,1)}, u32[]{:S(2)}) copy-start(bf16[4,256,128]{2,1,0:T(8,128)(2,1)} %get-tuple-element.34) | copy-start | bytes 786436
  84.8 40.1 %copy-start.10 = (bf16[4,256,128]{2,1,0:T(8,128)(2,1)S(1)}, bf16[4,256,128]{2,1,0:T(8,128)(2,1)}, u32[]{:S(2)}) copy-start(bf16[4,256,128]{2,1,0:T(8,128)(2,1)} %get-tuple-element.30) | copy-start | bytes 786436
  84.8 47.3 %copy-start.17 = (bf16[4,256,128]{2,1,0:T(8,128)(2,1)S(1)}, bf16[4,256,128]{2,1,0:T(8,128)(2,1)}, u32[]{:S(2)}) copy-start(bf16[4,256,128]{2,1,0:T(8,128)(2,1)} %get-tuple-element.29) | copy-start | bytes 786436
  84.8 10.8 %collective-permute-start.22 = (bf16[4,256,128]{2,1,0:T(8,128)(2,1)}, bf16[4,256,128]{2,1,0:T(8,128)(2,1)S(1)}, u32[]{:S(2)}, u32[]{:S(2)}) collective-permute-start(bf16[4,256,128]{2,1,0:T(8,128)(2,1)} %get-tuple-element.28), channel_id=1, source_target_pairs={{0,64},{8,72},{16,80},{24,88},{32,96},{40,104},{48,112},{56,120},{... | collective-permute-start | bytes 786440 | tf_op jit(solution)/shard_map/ppermute | solution.py:257
  85.9 11.0 %collective-permute-start.20 = (bf16[4,256,128]{2,1,0:T(8,128)(2,1)}, bf16[4,256,128]{2,1,0:T(8,128)(2,1)S(1)}, u32[]{:S(2)}, u32[]{:S(2)}) collective-permute-start(bf16[4,256,128]{2,1,0:T(8,128)(2,1)} %get-tuple-element.26), channel_id=1, source_target_pairs={{0,192},{8,200},{16,208},{24,216},{32,224},{40,232},{48,240},{56,2... | collective-permute-start | bytes 786440 | tf_op jit(solution)/shard_map/ppermute | solution.py:257
  90.0 10.7 %collective-permute-start.30 = (bf16[4,256,128]{2,1,0:T(8,128)(2,1)S(1)}, bf16[4,256,128]{2,1,0:T(8,128)(2,1)S(1)}, u32[]{:S(2)}, u32[]{:S(2)}) collective-permute-start(bf16[4,256,128]{2,1,0:T(8,128)(2,1)S(1)} %copy-done.19), channel_id=1, source_target_pairs={{0,56},{8,0},{16,8},{24,16},{32,24},{40,32},{48,40},{56,48},{64,12... | collective-permute-start | bytes 786440 | tf_op jit(solution)/shard_map/ppermute | solution.py:257
  90.7 10.9 %collective-permute-start.34 = (bf16[4,256,128]{2,1,0:T(8,128)(2,1)S(1)}, bf16[4,256,128]{2,1,0:T(8,128)(2,1)S(1)}, u32[]{:S(2)}, u32[]{:S(2)}) collective-permute-start(bf16[4,256,128]{2,1,0:T(8,128)(2,1)S(1)} %copy-done.18), channel_id=1, source_target_pairs={{0,8},{8,16},{16,24},{24,32},{32,40},{40,48},{48,56},{56,0},{64,72... | collective-permute-start | bytes 786440 | tf_op jit(solution)/shard_map/ppermute | solution.py:257
  95.7 16.5 %collective-permute-start.23 = (bf16[8,256,128]{2,1,0:T(8,128)(2,1)S(1)}, bf16[8,256,128]{2,1,0:T(8,128)(2,1)S(1)}, u32[]{:S(2)}, u32[]{:S(2)}) collective-permute-start(bf16[8,256,128]{2,1,0:T(8,128)(2,1)S(1)} %pad_maximum_fusion.1), channel_id=1, source_target_pairs={{0,64},{8,72},{16,80},{24,88},{32,96},{40,104},{48,112},{56,120},{... | collective-permute-start | bytes 1572872 | tf_op jit(solution)/shard_map/ppermute | solution.py:257
  97.1 15.2 %collective-permute-start.21 = (bf16[8,256,128]{2,1,0:T(8,128)(2,1)S(1)}, bf16[8,256,128]{2,1,0:T(8,128)(2,1)S(1)}, u32[]{:S(2)}, u32[]{:S(2)}) collective-permute-start(bf16[8,256,128]{2,1,0:T(8,128)(2,1)S(1)} %pad_maximum_fusion), channel_id=1, source_target_pairs={{0,192},{8,200},{16,208},{24,216},{32,224},{40,232},{48,240},{56,2... | collective-permute-start | bytes 1572872 | tf_op jit(solution)/shard_map/ppermute | solution.py:257
  100.8 9.2 %collective-permute-start.31 = (bf16[4,256,128]{2,1,0:T(8,128)(2,1)S(1)}, bf16[4,256,128]{2,1,0:T(8,128)(2,1)S(1)}, u32[]{:S(2)}, u32[]{:S(2)}) collective-permute-start(bf16[4,256,128]{2,1,0:T(8,128)(2,1)S(1)} %add_convert_fusion.4), channel_id=1, source_target_pairs={{0,56},{8,0},{16,8},{24,16},{32,24},{40,32},{48,40},{56,48},{64,12... | collective-permute-start | bytes 786440 | tf_op jit(solution)/shard_map/ppermute | solution.py:257
  101.7 10.7 %collective-permute-start.35 = (bf16[4,256,128]{2,1,0:T(8,128)(2,1)S(1)}, bf16[4,256,128]{2,1,0:T(8,128)(2,1)S(1)}, u32[]{:S(2)}, u32[]{:S(2)}) collective-permute-start(bf16[4,256,128]{2,1,0:T(8,128)(2,1)S(1)} %add_convert_fusion.1), channel_id=1, source_target_pairs={{0,8},{8,16},{16,24},{24,32},{32,40},{40,48},{48,56},{56,0},{64,72... | collective-permute-start | bytes 786440 | tf_op jit(solution)/shard_map/ppermute | solution.py:257
  110.1 14.8 %collective-permute-start.32 = (bf16[4,256,128]{2,1,0:T(8,128)(2,1)S(1)}, bf16[4,256,128]{2,1,0:T(8,128)(2,1)S(1)}, u32[]{:S(2)}, u32[]{:S(2)}) collective-permute-start(bf16[4,256,128]{2,1,0:T(8,128)(2,1)S(1)} %add_convert_fusion.3), channel_id=1, source_target_pairs={{0,56},{8,0},{16,8},{24,16},{32,24},{40,32},{48,40},{56,48},{64,12... | collective-permute-start | bytes 786440 | tf_op jit(solution)/shard_map/ppermute | solution.py:257
  112.4 10.7 %collective-permute-start.24 = (bf16[2,256,128]{2,1,0:T(8,128)(2,1)S(1)}, bf16[2,256,128]{2,1,0:T(8,128)(2,1)S(1)}, u32[]{:S(2)}, u32[]{:S(2)}) collective-permute-start(bf16[2,256,128]{2,1,0:T(8,128)(2,1)S(1)} %pad_maximum_fusion.4), channel_id=1, source_target_pairs={{0,48},{8,56},{16,0},{24,8},{32,16},{40,24},{48,32},{56,40},{64,11... | collective-permute-start | bytes 393224 | tf_op jit(solution)/shard_map/ppermute | solution.py:257
  112.5 18.6 %collective-permute-start.36 = (bf16[4,256,128]{2,1,0:T(8,128)(2,1)S(1)}, bf16[4,256,128]{2,1,0:T(8,128)(2,1)S(1)}, u32[]{:S(2)}, u32[]{:S(2)}) collective-permute-start(bf16[4,256,128]{2,1,0:T(8,128)(2,1)S(1)} %add_convert_fusion), channel_id=1, source_target_pairs={{0,8},{8,16},{16,24},{24,32},{32,40},{40,48},{48,56},{56,0},{64,72... | collective-permute-start | bytes 786440 | tf_op jit(solution)/shard_map/ppermute | solution.py:257
  123.2 6.7 %collective-permute-start.28 = (bf16[256,128]{1,0:T(8,128)(2,1)S(1)}, bf16[256,128]{1,0:T(8,128)(2,1)S(1)}, u32[]{:S(2)}, u32[]{:S(2)}) collective-permute-start(bf16[256,128]{1,0:T(8,128)(2,1)S(1)} %get-tuple-element.41), channel_id=1, source_target_pairs={{0,16},{8,24},{16,32},{24,40},{32,48},{40,56},{48,0},{56,8},{64,80... | collective-permute-start | bytes 196616 | tf_op jit(solution)/shard_map/ppermute | solution.py:257
  125.0 7.1 %collective-permute-start.33 = (bf16[4,256,128]{2,1,0:T(8,128)(2,1)S(1)}, bf16[4,256,128]{2,1,0:T(8,128)(2,1)S(1)}, u32[]{:S(2)}, u32[]{:S(2)}) collective-permute-start(bf16[4,256,128]{2,1,0:T(8,128)(2,1)S(1)} %add_convert_fusion.2), channel_id=1, source_target_pairs={{0,56},{8,0},{16,8},{24,16},{32,24},{40,32},{48,40},{56,48},{64,12... | collective-permute-start | bytes 786440 | tf_op jit(solution)/shard_map/ppermute | solution.py:257
  127.0 6.7 %collective-permute-start.25 = (bf16[256,128]{1,0:T(8,128)(2,1)S(1)}, bf16[256,128]{1,0:T(8,128)(2,1)S(1)}, u32[]{:S(2)}, u32[]{:S(2)}) collective-permute-start(bf16[256,128]{1,0:T(8,128)(2,1)S(1)} %get-tuple-element.39), channel_id=1, source_target_pairs={{0,56},{8,0},{16,8},{24,16},{32,24},{40,32},{48,40},{56,48},{64,12... | collective-permute-start | bytes 196616 | tf_op jit(solution)/shard_map/ppermute | solution.py:257
  128.2 6.1 %collective-permute-start.26 = (bf16[256,128]{1,0:T(8,128)(2,1)S(1)}, bf16[256,128]{1,0:T(8,128)(2,1)S(1)}, u32[]{:S(2)}, u32[]{:S(2)}) collective-permute-start(bf16[256,128]{1,0:T(8,128)(2,1)S(1)} %get-tuple-element.40), channel_id=1, source_target_pairs={{0,48},{8,56},{16,0},{24,8},{32,16},{40,24},{48,32},{56,40},{64,11... | collective-permute-start | bytes 196616 | tf_op jit(solution)/shard_map/ppermute | solution.py:257
  130.0 6.6 %collective-permute-start.27 = (bf16[256,128]{1,0:T(8,128)(2,1)S(1)}, bf16[256,128]{1,0:T(8,128)(2,1)S(1)}, u32[]{:S(2)}, u32[]{:S(2)}) collective-permute-start(bf16[256,128]{1,0:T(8,128)(2,1)S(1)} %get-tuple-element.42), channel_id=1, source_target_pairs={{0,16},{8,24},{16,32},{24,40},{32,48},{40,56},{48,0},{56,8},{64,80... | collective-permute-start | bytes 196616 | tf_op jit(solution)/shard_map/ppermute | solution.py:257
  131.2 6.6 %collective-permute-start.29 = (bf16[256,128]{1,0:T(8,128)(2,1)S(1)}, bf16[256,128]{1,0:T(8,128)(2,1)S(1)}, u32[]{:S(2)}, u32[]{:S(2)}) collective-permute-start(bf16[256,128]{1,0:T(8,128)(2,1)S(1)} %fusion.3), channel_id=1, source_target_pairs={{0,8},{8,16},{16,24},{24,32},{32,40},{40,48},{48,56},{56,0},{64,72... | collective-permute-start | bytes 196616 | tf_op jit(solution)/shard_map/ppermute | solution.py:257
  132.2 5.7 %collective-permute-start.37 = (bf16[256,128]{1,0:T(8,128)(2,1)S(1)}, bf16[256,128]{1,0:T(8,128)(2,1)S(1)}, u32[]{:S(2)}, u32[]{:S(2)}) collective-permute-start(bf16[256,128]{1,0:T(8,128)(2,1)S(1)} %get-tuple-element.45), channel_id=1, source_target_pairs={{0,192},{8,200},{16,208},{24,216},{32,224},{40,232},{48,240},{56,2... | collective-permute-start | bytes 196616 | tf_op jit(solution)/shard_map/ppermute | solution.py:257
  133.7 5.5 %collective-permute-start.39 = (bf16[256,128]{1,0:T(8,128)(2,1)S(1)}, bf16[256,128]{1,0:T(8,128)(2,1)S(1)}, u32[]{:S(2)}, u32[]{:S(2)}) collective-permute-start(bf16[256,128]{1,0:T(8,128)(2,1)S(1)} %get-tuple-element.46), channel_id=1, source_target_pairs={{0,64},{8,72},{16,80},{24,88},{32,96},{40,104},{48,112},{56,120},{... | collective-permute-start | bytes 196616 | tf_op jit(solution)/shard_map/ppermute | solution.py:257
  134.3 5.8 %collective-permute-start.38 = (bf16[256,128]{1,0:T(8,128)(2,1)S(1)}, bf16[256,128]{1,0:T(8,128)(2,1)S(1)}, u32[]{:S(2)}, u32[]{:S(2)}) collective-permute-start(bf16[256,128]{1,0:T(8,128)(2,1)S(1)} %get-tuple-element.47), channel_id=1, source_target_pairs={{0,128},{8,136},{16,144},{24,152},{32,160},{40,168},{48,176},{56,1... | collective-permute-start | bytes 196616 | tf_op jit(solution)/shard_map/ppermute | solution.py:257
Sparse Core Ops, SparseCore 0:
  84.9 43.8 reduce-scatter.1
